TPU v7x, 512 devices: a whole 4x4x16 slice. The times are simulated.
512 devices in a mesh: pipe: 16 (over z_lo, core), dp: 32 (over z_hi, y, x).
Axes of the slice: x: 4, y: 4, z: 16 (z_hi: 2, z_lo: 8; z = z_hi * 8 + z_lo), core: 2. Of those that a mesh axis runs over, the one named last changes fastest.
Arguments:
- queries: bfloat16 [16, 4096, 4096], P('pipe', 'dp'), may hold values from -8 to 8
- keys: bfloat16 [16, 4096, 512], P('pipe', 'dp'), may hold values from -8 to 8
- values: bfloat16 [16, 4096, 512], P('pipe', 'dp'), may hold values from -8 to 8
- block_pairs: int32 [16, 256, 2], P('pipe'), may hold values from 0 to 31, as said below
Outputs:
- attended: bfloat16 [16, 4096, 4096], P('pipe', 'dp')
Inputs may be any that keep to these rules, and one draw needn't show every extreme that they name: `block_pairs`: for each section, entries j * 8 to (j + 1) * 8 - 1 hold the pairs of query tile j (first element j); their key tiles are distinct and the first of them is j.
All inputs are finite; a program needn't handle non-finite values.
Results may differ from a plain program's by a relative error of at most 0.0047.
Values may be sent and summed in bfloat16 or wider, within the bound.
No kernel may reach another device: no remote copies, remote signals or barrier semaphores. Data moves between devices by JAX's collectives and lax.ppermute only.
A program may use at most 64 MiB of HBM per device.

v0:
```python
import math

import jax
import jax.numpy as jnp
from jax import lax
from jax.sharding import PartitionSpec as P

TILE_TOKENS = 128
QUERY_HEADS = 32
KEY_VALUE_HEADS = 4
HEAD_SIZE = 128


def passed_along(value, axis, steps):
    count = lax.axis_size(axis)
    pairs = [(source, (source + steps) % count) for source in range(count)]
    return lax.ppermute(value, axis, pairs)


def attend(queries_t, keys_t, values_t):
    scale = 1.0 / math.sqrt(HEAD_SIZE)
    scores = (
        jnp.einsum("brd,bld->brl", queries_t, keys_t, preferred_element_type=jnp.float32) * scale
    )
    largest = jnp.max(scores, axis=-1, keepdims=True)
    weights = jnp.exp(scores - largest)
    total = jnp.sum(weights, axis=-1, keepdims=True)
    rounded = weights.astype(jnp.bfloat16)
    mixed_rows = jnp.einsum("brl,bld->brd", rounded, values_t, preferred_element_type=jnp.float32)
    return (mixed_rows / total).astype(jnp.bfloat16)


def select_key_tiles(whole, chosen_tiles):
    tiles = whole.reshape(-1, TILE_TOKENS, whole.shape[-1])
    picked = jnp.take(tiles, chosen_tiles, axis=0)
    return picked.reshape(
        chosen_tiles.shape[0], chosen_tiles.shape[1] * TILE_TOKENS, whole.shape[-1]
    )


def local_rows(queries, every_key_row, every_value_row, chosen_tiles):
    block_count = chosen_tiles.shape[0]
    head_group = QUERY_HEADS // KEY_VALUE_HEADS
    query_head_rows = queries.reshape(
        block_count, TILE_TOKENS, KEY_VALUE_HEADS, head_group, HEAD_SIZE
    ).transpose(2, 0, 1, 3, 4)
    query_head_rows = query_head_rows.reshape(
        KEY_VALUE_HEADS, block_count, TILE_TOKENS * head_group, HEAD_SIZE
    )
    key_tile_rows = (
        select_key_tiles(every_key_row, chosen_tiles)
        .reshape(block_count, -1, KEY_VALUE_HEADS, HEAD_SIZE)
        .transpose(2, 0, 1, 3)
    )
    value_tile_rows = (
        select_key_tiles(every_value_row, chosen_tiles)
        .reshape(block_count, -1, KEY_VALUE_HEADS, HEAD_SIZE)
        .transpose(2, 0, 1, 3)
    )

    def one_head(operands):
        return attend(operands[0], operands[1], operands[2])

    mixed_rows = lax.map(one_head, (query_head_rows, key_tile_rows, value_tile_rows))
    mixed_rows = mixed_rows.reshape(
        KEY_VALUE_HEADS, block_count, TILE_TOKENS, head_group, HEAD_SIZE
    ).transpose(1, 2, 0, 3, 4)
    return mixed_rows.reshape(block_count * TILE_TOKENS, QUERY_HEADS * HEAD_SIZE)


def on_device(queries, keys, values, block_pairs):
    queries, keys, values = passed_along((queries, keys, values), "pipe", 1)
    tok_rows = keys.shape[1]
    all_blocks = tok_rows * lax.axis_size("dp") // TILE_TOKENS
    pairs = block_pairs[0]
    per_block = pairs.shape[0] // all_blocks
    chosen_all = pairs[:, 1].reshape(all_blocks, per_block)
    every_key_row, every_value_row = (
        lax.all_gather(keys, "dp", axis=1, tiled=True),
        lax.all_gather(values, "dp", axis=1, tiled=True),
    )
    own_blocks = tok_rows // TILE_TOKENS
    chosen_tiles = lax.dynamic_slice_in_dim(
        chosen_all, lax.axis_index("dp") * own_blocks, own_blocks, 0
    )
    mixed_rows = local_rows(queries[0], every_key_row[0], every_value_row[0], chosen_tiles)
    return mixed_rows[None]


def solution(mesh):
    placed = (
        P("pipe", "dp", None),
        P("pipe", "dp", None),
        P("pipe", "dp", None),
        P("pipe", None, None),
    )
    return jax.shard_map(
        on_device, mesh=mesh, in_specs=placed, out_specs=P("pipe", "dp", None), check_vma=False
    )
```

profile of v0, /device:TPU:6, one launch (start us, length us, event | category | flops | bytes accessed | tf_op | source)
XLA Modules:
  0.0 392.6 jit_solution(6080403995000779330)
XLA Ops:
  6.5 0.0 all-gather.3.cloned.1.call-start
  6.5 1.9 collective-permute-start.1
  8.5 13.5 %collective-permute-done.1 = bf16[1,128,512]{2,1,0:T(8,128)(2,1)S(1)} collective-permute-done((bf16[1,128,512]{2,1,0:T(8,128)(2,1)}, bf16[1,128,512]{2,1,0:T(8,128)(2,1)S(1)}, u32[]{:S(2)}, u32[]{:S(2)}) %collective-permute-start.1) | collective-permute-done | bytes 131104 | tf_op jit(solution)/shard_map/ppermute | solution.py:17
  22.0 0.0 copy-start.1
  22.0 0.6 copy-done.1
  22.6 0.0 all-gather.3.cloned.1.call-update
  22.7 0.0 all-gather.5.cloned.1.call-start
  22.7 1.9 collective-permute-start.2
  24.6 11.2 %collective-permute-done.2 = bf16[1,128,512]{2,1,0:T(8,128)(2,1)S(1)} collective-permute-done((bf16[1,128,512]{2,1,0:T(8,128)(2,1)}, bf16[1,128,512]{2,1,0:T(8,128)(2,1)S(1)}, u32[]{:S(2)}, u32[]{:S(2)}) %collective-permute-start.2) | collective-permute-done | bytes 131104 | tf_op jit(solution)/shard_map/ppermute | solution.py:17
  35.8 0.0 copy-start.2
  35.8 0.6 copy-done.2
  36.4 0.0 all-gather.5.cloned.1.call-update
  36.5 1.9 collective-permute-start
  38.4 0.7 slice_reduce_fusion
  39.1 0.1 reshape_squeeze.14
  39.2 23.9 %collective-permute-done = bf16[1,128,4096]{2,1,0:T(8,128)(2,1)S(1)} collective-permute-done((bf16[1,128,4096]{2,1,0:T(8,128)(2,1)}, bf16[1,128,4096]{2,1,0:T(8,128)(2,1)S(1)}, u32[]{:S(2)}, u32[]{:S(2)}) %collective-permute-start) | collective-permute-done | bytes 1048608 | tf_op jit(solution)/shard_map/ppermute | solution.py:17
  63.1 0.2 copy.21
  63.4 0.2 copy.24
  63.6 130.3 %all-gather.3.cloned.1.call-done = bf16[1,4096,512]{2,1,0:T(8,128)(2,1)} async-done(((bf16[1,128,512]{2,1,0:T(8,128)(2,1)}), bf16[1,4096,512]{2,1,0:T(8,128)(2,1)}) %all-gather.3.cloned.1.call-update) | async-done | bytes 4194320 | tf_op jit(solution)/shard_map/all_gather | solution.py:79
  193.9 2.8 gather_fusion
  196.7 163.0 %all-gather.5.cloned.1.call-done = bf16[1,4096,512]{2,1,0:T(8,128)(2,1)} async-done(((bf16[1,128,512]{2,1,0:T(8,128)(2,1)}), bf16[1,4096,512]{2,1,0:T(8,128)(2,1)}) %all-gather.5.cloned.1.call-update) | async-done | bytes 4194320 | tf_op jit(solution)/shard_map/all_gather | solution.py:80
  359.7 2.8 gather_fusion.1
  362.5 1.6 bitcast_select_fusion
  364.1 0.0 copy-start
  364.1 2.2 reshape.84
  366.3 1.6 copy.17
  368.0 0.0 copy-done
  368.0 1.1 reshape.85
  369.1 1.6 copy.18
  370.7 12.3 %while.10 = (s32[]{:T(128)}, bf16[4,1,1024,128]{3,2,1,0:T(8,128)(2,1)}, bf16[4,1,1024,128]{3,2,1,0:T(8,128)(2,1)S(1)}, bf16[4,1,1024,128]{2,3,0,1:T(8,128)(2,1)S...) while((s32[]{:T(128)}, bf16[4,1,1024,128]{3,2,1,0:T(8,128)(2,1)}, ...), condition=%wide.region_3.5_spmd, body=%wide.region_0.4_spmd.sunk | while | flops 545519616 | bytes 13654085 | solution.py:64
  370.7 0.8 multiply_reduce_fusion.2
  371.5 0.7 fusion.35
  372.2 1.6 fusion.36
  373.8 0.8 multiply_reduce_fusion.2
  374.6 0.7 fusion.35
  375.3 1.6 fusion.36
  376.9 0.8 multiply_reduce_fusion.2
  377.6 0.7 fusion.35
  378.4 1.6 fusion.36
  380.0 0.8 multiply_reduce_fusion.2
  380.7 0.7 fusion.35
  381.5 1.6 fusion.36
  383.0 1.4 copy_bitcast_fusion
  384.4 1.3 broadcast_in_dim_reshape.3
  (3 shorter events, 0.0 us)
Async XLA Ops:
  6.5 187.3 %all-gather.3.cloned.1.call-start = ((), (), s32[]{:S(2)}) async-start(), calls=%async_computation | async-start | bytes 4325376 | tf_op jit(solution)/shard_map/all_gather | solution.py:79
  6.5 15.4 %collective-permute-start.1 = (bf16[1,128,512]{2,1,0:T(8,128)(2,1)}, bf16[1,128,512]{2,1,0:T(8,128)(2,1)S(1)}, u32[]{:S(2)}, u32[]{:S(2)}) collective-permute-start(bf16[1,128,512]{2,1,0:T(8,128)(2,1)} %param.9), channel_id=1, source_target_pairs={{0,32},{32,64},{64,96},{96,128},{128,160},{160,192},{192,224},{224... | collective-permute-start | bytes 393224 | tf_op jit(solution)/shard_map/ppermute | solution.py:17
  22.0 0.6 copy-start.1
  22.7 337.0 %all-gather.5.cloned.1.call-start = ((), (), s32[]{:S(2)}) async-start(), calls=%async_computation.1 | async-start | bytes 4325376 | tf_op jit(solution)/shard_map/all_gather | solution.py:80
  22.7 13.1 %collective-permute-start.2 = (bf16[1,128,512]{2,1,0:T(8,128)(2,1)}, bf16[1,128,512]{2,1,0:T(8,128)(2,1)S(1)}, u32[]{:S(2)}, u32[]{:S(2)}) collective-permute-start(bf16[1,128,512]{2,1,0:T(8,128)(2,1)} %param.10), channel_id=1, source_target_pairs={{0,32},{32,64},{64,96},{96,128},{128,160},{160,192},{192,224},{224... | collective-permute-start | bytes 393224 | tf_op jit(solution)/shard_map/ppermute | solution.py:17
  35.8 0.6 copy-start.2
  36.5 26.6 %collective-permute-start = (bf16[1,128,4096]{2,1,0:T(8,128)(2,1)}, bf16[1,128,4096]{2,1,0:T(8,128)(2,1)S(1)}, u32[]{:S(2)}, u32[]{:S(2)}) collective-permute-start(bf16[1,128,4096]{2,1,0:T(8,128)(2,1)} %param.8), channel_id=1, source_target_pairs={{0,32},{32,64},{64,96},{96,128},{128,160},{160,192},{192,224},{224... | collective-permute-start | bytes 3145736 | tf_op jit(solution)/shard_map/ppermute | solution.py:17
  364.1 3.9 copy-start
Sparse Core Ops, SparseCore 0:
  22.8 171.0 all-gather.2
  198.2 161.4 all-gather.4
where the time goes:
time: 399 us; the launch traced here: 393 us
  waiting for transfers between devices  342 us (86%)
  local copies, waits for them, and re-layouts  17.3 us (4%)
  between operations  13.5 us (3%)
  matrix products  9.37 us (2%)
  starting transfers between devices  5.79 us (1%)
  other arithmetic  4.55 us (1%)
    all_gather x1, waiting for transfers between devices, on_device(): lax.all_gather(values, 'dp', axis=1, tiled=True)  163 us
    all_gather x1, waiting for transfers between devices, on_device(): lax.all_gather(keys, 'dp', axis=1, tiled=True)  130 us
    ppermute x3, waiting for transfers between devices, passed_along(): return lax.ppermute(value, axis, pairs)  48.6 us
  transfers between devices with their start and end apart: 5, of which 5 were waited for; matrix products, arithmetic and copies ran while one was open for 1% of the time, Pallas kernels for 0%

commit v1 on v0

v1 whole, which is shorter than its diff:
```python
import math

import jax
import jax.numpy as jnp
from jax import lax
from jax.experimental import pallas as pl
from jax.experimental.pallas import tpu as pltpu
from jax.sharding import PartitionSpec as P

TILE = 128
HEADS = 4
GROUP = 8
HEAD_SIZE = 128
PICKS = 8
WIDE = GROUP * HEAD_SIZE
SECTIONS = 16
SIDE = 4
PLANE = SIDE * SIDE
TILES = 2 * PLANE
AXES = ("pipe", "dp")
SCALE = math.log2(math.e) / math.sqrt(HEAD_SIZE)


def relayed(swap, turn):
    pairs = []
    for section in range(SECTIONS):
        for tile in range(TILES):
            half, row, column = tile // PLANE, tile // SIDE % SIDE, tile % SIDE
            target = (half ^ swap) * PLANE + (row + turn) % SIDE * SIDE + column
            pairs.append((section * TILES + tile, (section + 1) % SECTIONS * TILES + target))
    return pairs


def attention_kernel(slots, places, *refs):
    query_refs, kv_ref, out_ref = refs[:SIDE], refs[SIDE], refs[SIDE + 1]
    k_sel, v_sel = refs[SIDE + 2], refs[SIDE + 3]
    for turn in range(SIDE):
        for pick in range(PICKS):
            slot = slots[turn * PICKS + pick]
            rows = pl.ds(pick * TILE, TILE)
            k_sel[rows, :] = kv_ref[slot, :, :HEAD_SIZE]
            v_sel[rows, :] = kv_ref[slot, :, HEAD_SIZE:]
        for head in range(GROUP):
            columns = pl.ds(head * HEAD_SIZE, HEAD_SIZE)
            scores = lax.dot_general(
                query_refs[turn][:, columns], k_sel[...], (((1,), (1,)), ((), ())),
                preferred_element_type=jnp.float32,
            )
            largest = jnp.max(scores, axis=-1, keepdims=True)
            weights = jnp.exp2((scores - largest) * SCALE)
            total = jnp.sum(weights, axis=-1, keepdims=True)
            mixed = jnp.dot(
                weights.astype(jnp.bfloat16), v_sel[...], preferred_element_type=jnp.float32
            )
            out_ref[places[turn], :, columns] = (mixed / total).astype(jnp.bfloat16)


def attention(slots, places, queries, kv):
    vmem = pl.BlockSpec(memory_space=pltpu.VMEM)
    smem = pl.BlockSpec(memory_space=pltpu.SMEM)
    return pl.pallas_call(
        attention_kernel,
        out_shape=jax.ShapeDtypeStruct((SIDE, TILE, WIDE), jnp.bfloat16),
        in_specs=[smem, smem] + [vmem] * (SIDE + 1),
        out_specs=vmem,
        scratch_shapes=[
            pltpu.VMEM((PICKS * TILE, HEAD_SIZE), jnp.bfloat16),
            pltpu.VMEM((PICKS * TILE, HEAD_SIZE), jnp.bfloat16),
        ],
        compiler_params=pltpu.CompilerParams(vmem_limit_bytes=32 * 1024 * 1024),
        cost_estimate=pl.CostEstimate(
            flops=2 * 2 * SIDE * GROUP * TILE * PICKS * TILE * HEAD_SIZE,
            bytes_accessed=4 * 1024 * 1024,
            transcendentals=SIDE * GROUP * TILE * PICKS * TILE,
        ),
    )(slots, places, *queries, kv)


def on_device(queries, keys, values, block_pairs):
    queries, keys, values = queries[0], keys[0], values[0]
    place = lax.axis_index("dp")
    half, row, column = place // PLANE, place // SIDE % SIDE, place % SIDE
    groups_row = [[h * PLANE + y * SIDE + x for y in range(SIDE)] for h in range(2) for x in range(SIDE)]
    groups_plane = [[h * PLANE + i for i in range(PLANE)] for h in range(2)]

    def head_columns(array, head):
        return array[:, head * HEAD_SIZE : (head + 1) * HEAD_SIZE]

    kv = jnp.stack(
        [
            jnp.concatenate([head_columns(keys, h), head_columns(values, h)], axis=1)
            for h in range(HEADS)
        ]
    )
    far = lax.ppermute(kv, AXES, relayed(1, 0))
    near = lax.ppermute(kv, AXES, relayed(0, 0))
    pieces = [
        lax.ppermute(
            lax.dynamic_slice_in_dim(queries, (row + turn) % SIDE * WIDE, WIDE, 1),
            AXES,
            relayed(0, turn),
        )
        for turn in range(SIDE)
    ]
    both = jnp.stack([near, far], axis=1)
    sent = jnp.broadcast_to(both[:, None], (HEADS, SIDE) + both.shape[1:])
    sent = sent.reshape((PLANE, 2, TILE, 2 * HEAD_SIZE))
    landed = lax.all_to_all(sent, "dp", 0, 0, axis_index_groups=groups_plane)
    landed = landed.reshape(PLANE * 2, TILE, 2 * HEAD_SIZE)

    places = (row - jnp.arange(SIDE, dtype=jnp.int32)) % SIDE
    blocks = half * PLANE + places * SIDE + column
    chosen = jnp.take(block_pairs[0, :, 1].reshape(TILES, PICKS), blocks, axis=0)
    slots = (chosen % PLANE) * 2 + ((chosen // PLANE) ^ half)
    mixed = attention(slots.reshape(-1).astype(jnp.int32), places, pieces, landed)
    back = lax.all_to_all(mixed, "dp", 0, 0, axis_index_groups=groups_row)
    return jnp.concatenate([back[h] for h in range(HEADS)], axis=1)[None]


def solution(mesh):
    placed = (
        P("pipe", "dp", None),
        P("pipe", "dp", None),
        P("pipe", "dp", None),
        P("pipe", None, None),
    )
    return jax.shard_map(
        on_device, mesh=mesh, in_specs=placed, out_specs=P("pipe", "dp", None), check_vma=False
    )
```

time: 399 us -> 126 us (0.32)
  the two profiles are of different devices: /device:TPU:6 before, /device:TPU:66 now
where the time goes in v1:
time: 126 us
  waiting for transfers between devices  51.1 us (41%)
  starting transfers between devices  36.9 us (29%)
  blocking collectives  19.1 us (15%)
  Pallas kernels  11.9 us (9%)
  local copies, waits for them, and re-layouts  4.98 us (4%)
  other arithmetic  1.31 us (1%)
    ppermute x1, waiting for transfers between devices, on_device(): far = lax.ppermute(kv, AXES, relayed(1, 0))  27.8 us
    all_to_all x1, blocking collectives, on_device(): back = lax.all_to_all(mixed, 'dp', 0, 0, axis_index_groups=groups_row)  19.1 us
    ppermute x4, waiting for transfers between devices, on_device(): lax.ppermute(lax.dynamic_slice_in_dim(queries, (row + turn) % SIDE * WIDE...  16.9 us
    ppermute x4, starting transfers between devices, on_device(): lax.ppermute(lax.dynamic_slice_in_dim(queries, (row + turn) % SIDE * WIDE...  13.7 us
    ppermute x1, starting transfers between devices, on_device(): far = lax.ppermute(kv, AXES, relayed(1, 0))  13.4 us
    pallas_call x1, Pallas kernels, attention(): pl.pallas_call(attention_kernel, out_shape=jax.ShapeDtypeStruct((SIDE, TI...  11.9 us
    all_to_all x1, starting transfers between devices, on_device(): landed = lax.all_to_all(sent, 'dp', 0, 0, axis_index_groups=groups_plane)  7.61 us
    all_to_all x1, waiting for transfers between devices, on_device(): landed = lax.all_to_all(sent, 'dp', 0, 0, axis_index_groups=groups_plane)  6.46 us
  transfers between devices with their start and end apart: 7, of which 4 were waited for; matrix products, arithmetic and copies ran while one was open for 1% of the time, Pallas kernels for 0%

profile of v1, /device:TPU:66, one launch (start us, length us, event | category | flops | bytes accessed | tf_op | source)
XLA Modules:
  0.0 125.5 jit_solution(9833919237239906513)
XLA Ops:
  0.0 0.8 fusion.8
  0.8 0.8 fusion.9
  1.7 13.4 %collective-permute-start.5 = (bf16[4,128,256]{2,1,0:T(8,128)(2,1)S(1)}, bf16[4,128,256]{2,1,0:T(8,128)(2,1)S(1)}, u32[]{:S(2)}, u32[]{:S(2)}) collective-permute-start(bf16[4,128,256]{2,1,0:T(8,128)(2,1)S(1)} %pad_maximum_fusion.1), channel_id=1, source_target_pairs={{0,48},{1,49},{2,50},{3,51},{4,52},{5,53},{6,54},{7,55},{8,56},{9,... | collective-permute-start | bytes 786440 | tf_op jit(solution)/shard_map/ppermute | solution.py:95
  15.1 2.1 %collective-permute-start.4 = (bf16[4,128,256]{2,1,0:T(8,128)(2,1)S(1)}, bf16[4,128,256]{2,1,0:T(8,128)(2,1)S(1)}, u32[]{:S(2)}, u32[]{:S(2)}) collective-permute-start(bf16[4,128,256]{2,1,0:T(8,128)(2,1)S(1)} %pad_maximum_fusion.1), channel_id=1, source_target_pairs={{0,32},{1,33},{2,34},{3,35},{4,36},{5,37},{6,38},{7,39},{8,40},{9,... | collective-permute-start | bytes 786440 | tf_op jit(solution)/shard_map/ppermute | solution.py:96
  17.3 27.8 %collective-permute-done.5 = bf16[4,128,256]{2,1,0:T(8,128)(2,1)S(1)} collective-permute-done((bf16[4,128,256]{2,1,0:T(8,128)(2,1)S(1)}, bf16[4,128,256]{2,1,0:T(8,128)(2,1)S(1)}, u32[]{:S(2)}, u32[]{:S(2)}) %collective-permute-start.5) | collective-permute-done | bytes 262176 | tf_op jit(solution)/shard_map/ppermute | solution.py:95
  45.1 0.0 collective-permute-done.4
  45.1 0.1 pad_maximum_fusion
  45.2 1.6 %broadcast_in_dim.21 = bf16[4,4,2,128,256]{4,3,2,1,0:T(8,128)(2,1)} broadcast(bf16[4,2,128,256]{3,2,1,0:T(8,128)(2,1)S(1)} %copy.6), dimensions={0,2,3,4} | broadcast | bytes 2621440 | tf_op jit(solution)/shard_map/broadcast_in_dim | solution.py:106
  46.7 0.0 copy-start
  46.8 7.6 %all-to-all-start = ((bf16[16,2,128,256]{3,2,1,0:T(8,128)(2,1)}), bf16[16,2,128,256]{3,2,1,0:T(8,128)(2,1)S(1)}, u32[]{:S(2)}, u32[]{:S(2)}) async-start(bf16[16,2,128,256]{3,2,1,0:T(8,128)(2,1)} %bitcast.35), calls=%async_computation | async-start | bytes 4194304 | tf_op jit(solution)/shard_map/all_to_all | solution.py:108
  54.4 0.0 copy-start.1
  54.5 0.0 copy-done
  54.5 0.9 dynamic-slice_bitcast_fusion
  55.4 4.6 %collective-permute-start.3 = (bf16[128,1024]{1,0:T(8,128)(2,1)}, bf16[128,1024]{1,0:T(8,128)(2,1)S(1)}, u32[]{:S(2)}, u32[]{:S(2)}) collective-permute-start(bf16[128,1024]{1,0:T(8,128)(2,1)} %get-tuple-element.9), channel_id=1, source_target_pairs={{0,44},{1,45},{2,46},{3,47},{4,32},{5,33},{6,34},{7,35},{8,36},{9,... | collective-permute-start | bytes 786440 | tf_op jit(solution)/shard_map/ppermute | solution.py:98
  60.0 2.7 %collective-permute-start.1 = (bf16[128,1024]{1,0:T(8,128)(2,1)}, bf16[128,1024]{1,0:T(8,128)(2,1)S(1)}, u32[]{:S(2)}, u32[]{:S(2)}) collective-permute-start(bf16[128,1024]{1,0:T(8,128)(2,1)} %get-tuple-element.10), channel_id=1, source_target_pairs={{0,36},{1,37},{2,38},{3,39},{4,40},{5,41},{6,42},{7,43},{8,44},{9,... | collective-permute-start | bytes 786440 | tf_op jit(solution)/shard_map/ppermute | solution.py:98
  62.7 3.0 %collective-permute-start = (bf16[128,1024]{1,0:T(8,128)(2,1)}, bf16[128,1024]{1,0:T(8,128)(2,1)S(1)}, u32[]{:S(2)}, u32[]{:S(2)}) collective-permute-start(bf16[128,1024]{1,0:T(8,128)(2,1)} %get-tuple-element.11), channel_id=1, source_target_pairs={{0,32},{1,33},{2,34},{3,35},{4,36},{5,37},{6,38},{7,39},{8,40},{9,... | collective-permute-start | bytes 786440 | tf_op jit(solution)/shard_map/ppermute | solution.py:98
  65.7 3.5 %collective-permute-start.2 = (bf16[128,1024]{1,0:T(8,128)(2,1)S(1)}, bf16[128,1024]{1,0:T(8,128)(2,1)S(1)}, u32[]{:S(2)}, u32[]{:S(2)}) collective-permute-start(bf16[128,1024]{1,0:T(8,128)(2,1)S(1)} %get-tuple-element.12), channel_id=1, source_target_pairs={{0,40},{1,41},{2,42},{3,43},{4,44},{5,45},{6,46},{7,47},{8,32},{9,... | collective-permute-start | bytes 786440 | tf_op jit(solution)/shard_map/ppermute | solution.py:98
  69.2 0.0 copy-done.1
  69.2 0.1 reshape_squeeze.3
  69.3 0.6 gather_fusion
  69.9 0.1 broadcast_select_fusion
  70.0 0.1 select_n.100
  70.1 16.3 %collective-permute-done.3.refs_3_ = bf16[128,1024]{1,0:T(8,128)(2,1)S(1)} collective-permute-done((bf16[128,1024]{1,0:T(8,128)(2,1)}, bf16[128,1024]{1,0:T(8,128)(2,1)S(1)}, u32[]{:S(2)}, u32[]{:S(2)}) %collective-permute-start.3) | collective-permute-done | bytes 262176 | tf_op jit(solution)/shard_map/ppermute | solution.py:98
  86.4 0.0 collective-permute-done.1.refs_1_
  86.4 0.0 collective-permute-done.refs_0_
  86.4 0.5 collective-permute-done.2.refs_2_
  87.0 6.5 %all-to-all-done = bf16[16,2,128,256]{3,2,1,0:T(8,128)(2,1)S(1)} async-done(((bf16[16,2,128,256]{3,2,1,0:T(8,128)(2,1)}), bf16[16,2,128,256]{3,2,1,0:T(8,128)(2,1)S(1)}, u32[]{:S(2)}, u32[]{:S(2)}) %all-to-all-start) | async-done | bytes 2097184 | tf_op jit(solution)/shard_map/all_to_all | solution.py:108
  93.4 11.9 %shard_map.46 = bf16[4,128,1024]{2,1,0:T(8,128)(2,1)S(1)} custom-call(s32[32]{0:T(128)S(1)} %fusion.4.slots, s32[4]{0:T(128)S(1)} %and_select_fusion.3.places, bf16[128,1024]{1,0:T(8,128)(2,1)S(1)} %collective-permute-done.refs_0_, bf16[128,1024]{1,0:T(8,128)(2,1)S(1)} %collective-permute-done.1.refs_1_, ...), custom_call_target="tpu_custom_call" | custom-call | flops 2147483648 | bytes 4194304 | tf_op jit(solution)/shard_map/pallas_call | solution.py:61
  105.4 19.1 %all_to_all.10 = bf16[4,128,1024]{2,1,0:T(8,128)(2,1)S(1)} all-to-all(bf16[4,128,1024]{2,1,0:T(8,128)(2,1)S(1)} %shard_map.46), channel_id=1, replica_groups={{0,4,8,12},{1,5,9,13},{2,6,10,14},{3,7,11,15},{16,20,24,28},{17,21,25,2..., dimensions={0} | all-to-all | bytes 2097152 | tf_op jit(solution)/shard_map/all_to_all | solution.py:116
  124.4 0.1 slice_bitcast_fusion.3
  124.5 1.0 maximum_bitcast_fusion
  (10 shorter events, 0.2 us)
Async XLA Ops:
  1.7 43.3 %collective-permute-start.5 = (bf16[4,128,256]{2,1,0:T(8,128)(2,1)S(1)}, bf16[4,128,256]{2,1,0:T(8,128)(2,1)S(1)}, u32[]{:S(2)}, u32[]{:S(2)}) collective-permute-start(bf16[4,128,256]{2,1,0:T(8,128)(2,1)S(1)} %pad_maximum_fusion.1), channel_id=1, source_target_pairs={{0,48},{1,49},{2,50},{3,51},{4,52},{5,53},{6,54},{7,55},{8,56},{9,... | collective-permute-start | bytes 786440 | tf_op jit(solution)/shard_map/ppermute | solution.py:95
  15.1 29.9 %collective-permute-start.4 = (bf16[4,128,256]{2,1,0:T(8,128)(2,1)S(1)}, bf16[4,128,256]{2,1,0:T(8,128)(2,1)S(1)}, u32[]{:S(2)}, u32[]{:S(2)}) collective-permute-start(bf16[4,128,256]{2,1,0:T(8,128)(2,1)S(1)} %pad_maximum_fusion.1), channel_id=1, source_target_pairs={{0,32},{1,33},{2,34},{3,35},{4,36},{5,37},{6,38},{7,39},{8,40},{9,... | collective-permute-start | bytes 786440 | tf_op jit(solution)/shard_map/ppermute | solution.py:96
  46.7 7.7 %copy-start = (bf16[1,128,4096]{2,1,0:T(8,128)(2,1)S(1)}, bf16[1,128,4096]{2,1,0:T(8,128)(2,1)}, u32[]{:S(2)}) copy-start(bf16[1,128,4096]{2,1,0:T(8,128)(2,1)} %param.4) | copy-start | bytes 3145732
  46.8 46.7 %all-to-all-start = ((bf16[16,2,128,256]{3,2,1,0:T(8,128)(2,1)}), bf16[16,2,128,256]{3,2,1,0:T(8,128)(2,1)S(1)}, u32[]{:S(2)}, u32[]{:S(2)}) async-start(bf16[16,2,128,256]{3,2,1,0:T(8,128)(2,1)} %bitcast.35), calls=%async_computation | async-start | bytes 4194304 | tf_op jit(solution)/shard_map/all_to_all | solution.py:108
  54.4 14.8 %copy-start.1 = (s32[1,256,2]{1,2,0:T(2,128)S(1)}, s32[1,256,2]{1,2,0:T(2,128)}, u32[]{:S(2)}) copy-start(s32[1,256,2]{1,2,0:T(2,128)} %param.7) | copy-start | bytes 6148
  55.4 31.0 %collective-permute-start.3 = (bf16[128,1024]{1,0:T(8,128)(2,1)}, bf16[128,1024]{1,0:T(8,128)(2,1)S(1)}, u32[]{:S(2)}, u32[]{:S(2)}) collective-permute-start(bf16[128,1024]{1,0:T(8,128)(2,1)} %get-tuple-element.9), channel_id=1, source_target_pairs={{0,44},{1,45},{2,46},{3,47},{4,32},{5,33},{6,34},{7,35},{8,36},{9,... | collective-permute-start | bytes 786440 | tf_op jit(solution)/shard_map/ppermute | solution.py:98
  60.0 26.4 %collective-permute-start.1 = (bf16[128,1024]{1,0:T(8,128)(2,1)}, bf16[128,1024]{1,0:T(8,128)(2,1)S(1)}, u32[]{:S(2)}, u32[]{:S(2)}) collective-permute-start(bf16[128,1024]{1,0:T(8,128)(2,1)} %get-tuple-element.10), channel_id=1, source_target_pairs={{0,36},{1,37},{2,38},{3,39},{4,40},{5,41},{6,42},{7,43},{8,44},{9,... | collective-permute-start | bytes 786440 | tf_op jit(solution)/shard_map/ppermute | solution.py:98
  62.7 23.7 %collective-permute-start = (bf16[128,1024]{1,0:T(8,128)(2,1)}, bf16[128,1024]{1,0:T(8,128)(2,1)S(1)}, u32[]{:S(2)}, u32[]{:S(2)}) collective-permute-start(bf16[128,1024]{1,0:T(8,128)(2,1)} %get-tuple-element.11), channel_id=1, source_target_pairs={{0,32},{1,33},{2,34},{3,35},{4,36},{5,37},{6,38},{7,39},{8,40},{9,... | collective-permute-start | bytes 786440 | tf_op jit(solution)/shard_map/ppermute | solution.py:98
  65.7 21.3 %collective-permute-start.2 = (bf16[128,1024]{1,0:T(8,128)(2,1)S(1)}, bf16[128,1024]{1,0:T(8,128)(2,1)S(1)}, u32[]{:S(2)}, u32[]{:S(2)}) collective-permute-start(bf16[128,1024]{1,0:T(8,128)(2,1)S(1)} %get-tuple-element.12), channel_id=1, source_target_pairs={{0,40},{1,41},{2,42},{3,43},{4,44},{5,45},{6,46},{7,47},{8,32},{9,... | collective-permute-start | bytes 786440 | tf_op jit(solution)/shard_map/ppermute | solution.py:98

commit v2 on v1

v2 whole, which is shorter than its diff:
```python
import math

import jax
import jax.numpy as jnp
from jax import lax
from jax.experimental import pallas as pl
from jax.experimental.pallas import tpu as pltpu
from jax.sharding import PartitionSpec as P

TILE = 128
HEADS = 4
GROUP = 8
HEAD_SIZE = 128
PICKS = 8
WIDE = GROUP * HEAD_SIZE
SECTIONS = 16
SIDE = 4
PLANE = SIDE * SIDE
TILES = 2 * PLANE
AXES = ("pipe", "dp")
SCALE = math.log2(math.e) / math.sqrt(HEAD_SIZE)
VMEM = pl.BlockSpec(memory_space=pltpu.VMEM)
SMEM = pl.BlockSpec(memory_space=pltpu.SMEM)


def route(step, swap, turn):
    pairs = []
    for section in range(SECTIONS):
        for tile in range(TILES):
            half, row, column = tile // PLANE, tile // SIDE % SIDE, tile % SIDE
            target = (half ^ swap) * PLANE + (row + turn) % SIDE * SIDE + column
            pairs.append((section * TILES + tile, (section + step) % SECTIONS * TILES + target))
    return pairs


def attention_kernel(slots, query_ref, near_ref, far_ref, out_ref, k_sel, v_sel):
    for pick in range(PICKS):
        slot = slots[pick]
        rows = pl.ds(pick * TILE, TILE)
        for side, held in enumerate((near_ref, far_ref)):

            @pl.when(slot // PLANE == side)
            def _():
                k_sel[rows, :] = held[slot % PLANE, :, :HEAD_SIZE]
                v_sel[rows, :] = held[slot % PLANE, :, HEAD_SIZE:]

    for head in range(GROUP):
        columns = pl.ds(head * HEAD_SIZE, HEAD_SIZE)
        scores = lax.dot_general(
            query_ref[:, columns], k_sel[...], (((1,), (1,)), ((), ())),
            preferred_element_type=jnp.float32,
        )
        largest = jnp.max(scores, axis=-1, keepdims=True)
        weights = jnp.exp2((scores - largest) * SCALE)
        total = jnp.sum(weights, axis=-1, keepdims=True)
        mixed = jnp.dot(
            weights.astype(jnp.bfloat16), v_sel[...], preferred_element_type=jnp.float32
        )
        out_ref[:, columns] = (mixed / total).astype(jnp.bfloat16)


def attention(slots, queries, near, far):
    return pl.pallas_call(
        attention_kernel,
        out_shape=jax.ShapeDtypeStruct((TILE, WIDE), jnp.bfloat16),
        in_specs=[SMEM, VMEM, VMEM, VMEM],
        out_specs=VMEM,
        scratch_shapes=[
            pltpu.VMEM((PICKS * TILE, HEAD_SIZE), jnp.bfloat16),
            pltpu.VMEM((PICKS * TILE, HEAD_SIZE), jnp.bfloat16),
        ],
        compiler_params=pltpu.CompilerParams(vmem_limit_bytes=32 * 1024 * 1024),
        cost_estimate=pl.CostEstimate(
            flops=2 * 2 * GROUP * TILE * PICKS * TILE * HEAD_SIZE,
            bytes_accessed=1024 * 1024,
            transcendentals=GROUP * TILE * PICKS * TILE,
        ),
    )(slots, queries, near, far)


def assemble_kernel(heads, *refs):
    for turn in range(SIDE):
        start = pl.multiple_of(heads[turn] * WIDE, WIDE)
        refs[SIDE][:, pl.ds(start, WIDE)] = refs[turn][...]


def assemble(heads, pieces):
    return pl.pallas_call(
        assemble_kernel,
        out_shape=jax.ShapeDtypeStruct((TILE, HEADS * WIDE), jnp.bfloat16),
        in_specs=[SMEM] + [VMEM] * SIDE,
        out_specs=VMEM,
        compiler_params=pltpu.CompilerParams(vmem_limit_bytes=16 * 1024 * 1024),
        cost_estimate=pl.CostEstimate(flops=0, bytes_accessed=2 * 1024 * 1024, transcendentals=0),
    )(heads, *pieces)


def on_device(queries, keys, values, block_pairs):
    queries, keys, values = queries[0], keys[0], values[0]
    place = lax.axis_index("dp")
    half, row, column = place // PLANE, place // SIDE % SIDE, place % SIDE
    groups = [[h * PLANE + i for i in range(PLANE)] for h in range(2)]

    def head_columns(array, head):
        return array[:, head * HEAD_SIZE : (head + 1) * HEAD_SIZE]

    def spread(held):
        sent = jnp.broadcast_to(held[:, None], (HEADS, SIDE) + held.shape[1:])
        sent = sent.reshape((PLANE,) + held.shape[1:])
        return lax.all_to_all(sent, "dp", 0, 0, axis_index_groups=groups)

    kv = jnp.stack(
        [
            jnp.concatenate([head_columns(keys, h), head_columns(values, h)], axis=1)
            for h in range(HEADS)
        ]
    )
    far = lax.ppermute(kv, AXES, route(0, 1, 0))
    near_landed = spread(kv)
    pairs = lax.ppermute(block_pairs[0, :, 1].reshape(TILES, PICKS), AXES, route(-1, 0, 0))
    heads = (row + jnp.arange(SIDE, dtype=jnp.int32)) % SIDE
    pieces = [lax.dynamic_slice_in_dim(queries, heads[turn] * WIDE, WIDE, 1) for turn in range(SIDE)]
    for turn in range(1, SIDE):
        pieces[turn] = lax.ppermute(pieces[turn], AXES, route(0, 0, turn))
    far, near_landed, pairs, *pieces = lax.optimization_barrier((far, near_landed, pairs, *pieces))
    far_landed = spread(far)

    blocks = half * PLANE + (row - jnp.arange(SIDE, dtype=jnp.int32)) % SIDE * SIDE + column
    chosen = jnp.take(pairs, blocks, axis=0)
    slots = (chosen % PLANE) + ((chosen // PLANE) ^ half) * PLANE
    back = [None] * SIDE
    for turn in (2, 1, 3, 0):
        mixed = attention(slots[turn], pieces[turn], near_landed, far_landed)
        back[turn] = lax.ppermute(mixed, AXES, route(1, 0, -turn))
    return assemble(heads, back)[None]


def solution(mesh):
    placed = (
        P("pipe", "dp", None),
        P("pipe", "dp", None),
        P("pipe", "dp", None),
        P("pipe", None, None),
    )
    return jax.shard_map(
        on_device, mesh=mesh, in_specs=placed, out_specs=P("pipe", "dp", None), check_vma=False
    )
```

time: 126 us -> 115 us (0.913)
  the two profiles are of different devices: /device:TPU:66 before, /device:TPU:6 now
where the time goes in v2:
time: 115 us; the launch traced here: 113 us
  starting transfers between devices  52.3 us (45%)
  waiting for transfers between devices  36.2 us (31%)
  Pallas kernels  16.6 us (14%)
  local copies, waits for them, and re-layouts  5.33 us (5%)
  between operations  2.68 us (2%)
    all_to_all x2, waiting for transfers between devices, spread(): return lax.all_to_all(sent, 'dp', 0, 0, axis_index_groups=groups)  15.9 us
    pallas_call x4, Pallas kernels, attention(): pl.pallas_call(attention_kernel, out_shape=jax.ShapeDtypeStruct((TILE, WI...  15 us
    all_to_all x2, starting transfers between devices, spread(): return lax.all_to_all(sent, 'dp', 0, 0, axis_index_groups=groups)  14.3 us
    ppermute x4, waiting for transfers between devices, on_device(): back[turn] = lax.ppermute(mixed, AXES, route(1, 0, -turn))  14.1 us
    ppermute x1, starting transfers between devices, on_device(): far = lax.ppermute(kv, AXES, route(0, 1, 0))  13.8 us
    ppermute x3, starting transfers between devices, on_device(): pieces[turn] = lax.ppermute(pieces[turn], AXES, route(0, 0, turn))  10.8 us
    ppermute x4, starting transfers between devices, on_device(): back[turn] = lax.ppermute(mixed, AXES, route(1, 0, -turn))  9.97 us
    ppermute x3, waiting for transfers between devices, on_device(): pieces[turn] = lax.ppermute(pieces[turn], AXES, route(0, 0, turn))  4.75 us
  transfers between devices with their start and end apart: 11, of which 5 were waited for; matrix products, arithmetic and copies ran while one was open for 2% of the time, Pallas kernels for 10%

profile of v2, /device:TPU:6, one launch (start us, length us, event | category | flops | bytes accessed | tf_op | source)
XLA Modules:
  0.0 113.4 jit_solution(4360961573379456917)
XLA Ops:
  0.0 0.0 copy-start.1
  0.0 0.9 fusion.15
  0.9 0.1 copy-done.1
  1.1 1.1 broadcast_in_dim.26
  2.2 0.0 copy-start
  2.2 9.4 %all-to-all-start = ((bf16[16,128,256]{2,1,0:T(8,128)(2,1)}), bf16[16,128,256]{2,1,0:T(8,128)(2,1)S(1)}, u32[]{:S(2)}, u32[]{:S(2)}) async-start(bf16[16,128,256]{2,1,0:T(8,128)(2,1)} %bitcast.6), calls=%async_computation | async-start | bytes 2097152 | tf_op jit(solution)/shard_map/all_to_all | solution.py:110
  11.6 13.8 %collective-permute-start = (bf16[4,128,256]{2,1,0:T(8,128)(2,1)S(1)}, bf16[4,128,256]{2,1,0:T(8,128)(2,1)S(1)}, u32[]{:S(2)}, u32[]{:S(2)}) collective-permute-start(bf16[4,128,256]{2,1,0:T(8,128)(2,1)S(1)} %pad_maximum_fusion), channel_id=1, source_target_pairs={{0,16},{1,17},{2,18},{3,19},{4,20},{5,21},{6,22},{7,23},{8,24},{9,... | collective-permute-start | bytes 786440 | tf_op jit(solution)/shard_map/ppermute | solution.py:118
  25.5 0.6 fusion.17
  28.6 0.0 copy-done
  28.6 0.9 dynamic-slice_bitcast_fusion
  29.5 0.0 copy-start.2
  29.5 4.7 %collective-permute-start.4 = (bf16[128,1024]{1,0:T(8,128)(2,1)}, bf16[128,1024]{1,0:T(8,128)(2,1)S(1)}, u32[]{:S(2)}, u32[]{:S(2)}) collective-permute-start(bf16[128,1024]{1,0:T(8,128)(2,1)} %get-tuple-element.19), channel_id=1, source_target_pairs={{0,12},{1,13},{2,14},{3,15},{4,0},{5,1},{6,2},{7,3},{8,4},{9,5},{1... | collective-permute-start | bytes 786440 | tf_op jit(solution)/shard_map/ppermute | solution.py:124
  34.2 1.9 %collective-permute-start.2 = (bf16[128,1024]{1,0:T(8,128)(2,1)}, bf16[128,1024]{1,0:T(8,128)(2,1)S(1)}, u32[]{:S(2)}, u32[]{:S(2)}) collective-permute-start(bf16[128,1024]{1,0:T(8,128)(2,1)} %get-tuple-element.20), channel_id=1, source_target_pairs={{0,4},{1,5},{2,6},{3,7},{4,8},{5,9},{6,10},{7,11},{8,12},{9,13},{1... | collective-permute-start | bytes 786440 | tf_op jit(solution)/shard_map/ppermute | solution.py:124
  36.1 4.2 %collective-permute-start.3 = (bf16[128,1024]{1,0:T(8,128)(2,1)S(1)}, bf16[128,1024]{1,0:T(8,128)(2,1)S(1)}, u32[]{:S(2)}, u32[]{:S(2)}) collective-permute-start(bf16[128,1024]{1,0:T(8,128)(2,1)S(1)} %get-tuple-element.22), channel_id=1, source_target_pairs={{0,8},{1,9},{2,10},{3,11},{4,12},{5,13},{6,14},{7,15},{8,0},{9,1},... | collective-permute-start | bytes 786440 | tf_op jit(solution)/shard_map/ppermute | solution.py:124
  40.3 0.0 copy-done.2
  40.4 0.1 reshape_squeeze.3
  40.5 3.4 %collective-permute-start.1 = (s32[32,8]{1,0:T(8,128)S(1)}, s32[32,8]{1,0:T(8,128)S(1)}, u32[]{:S(2)}, u32[]{:S(2)}) collective-permute-start(s32[32,8]{1,0:T(8,128)S(1)} %reshape_squeeze.3), channel_id=1, source_target_pairs={{0,480},{1,481},{2,482},{3,483},{4,484},{5,485},{6,486},{7,487},{8... | collective-permute-start | bytes 3080 | tf_op jit(solution)/shard_map/ppermute | solution.py:120
  43.9 1.4 %collective-permute-done.1 = s32[32,8]{1,0:T(8,128)S(1)} collective-permute-done((s32[32,8]{1,0:T(8,128)S(1)}, s32[32,8]{1,0:T(8,128)S(1)}, u32[]{:S(2)}, u32[]{:S(2)}) %collective-permute-start.1) | collective-permute-done | bytes 1056 | tf_op jit(solution)/shard_map/ppermute | solution.py:120
  45.3 0.0 collective-permute-done
  45.3 0.0 collective-permute-done.4.query_ref
  45.3 4.7 %collective-permute-done.2.query_ref = bf16[128,1024]{1,0:T(8,128)(2,1)S(1)} collective-permute-done((bf16[128,1024]{1,0:T(8,128)(2,1)}, bf16[128,1024]{1,0:T(8,128)(2,1)S(1)}, u32[]{:S(2)}, u32[]{:S(2)}) %collective-permute-start.2) | collective-permute-done | bytes 262176 | tf_op jit(solution)/shard_map/ppermute | solution.py:124
  50.0 0.0 collective-permute-done.3.query_ref
  50.1 0.0 all-to-all-done.near_ref
  50.1 1.1 broadcast_in_dim.28
  51.1 4.8 %all-to-all-start.1 = ((bf16[16,128,256]{2,1,0:T(8,128)(2,1)}), bf16[16,128,256]{2,1,0:T(8,128)(2,1)S(1)}, u32[]{:S(2)}, u32[]{:S(2)}) async-start(bf16[16,128,256]{2,1,0:T(8,128)(2,1)} %bitcast.35), calls=%async_computation.1 | async-start | bytes 2097152 | tf_op jit(solution)/shard_map/all_to_all | solution.py:110
  56.0 0.6 gather_fusion
  56.6 0.1 fusion
  56.7 15.9 %all-to-all-done.1.far_ref = bf16[16,128,256]{2,1,0:T(8,128)(2,1)S(1)} async-done(((bf16[16,128,256]{2,1,0:T(8,128)(2,1)}), bf16[16,128,256]{2,1,0:T(8,128)(2,1)S(1)}, u32[]{:S(2)}, u32[]{:S(2)}) %all-to-all-start.1) | async-done | bytes 1048608 | tf_op jit(solution)/shard_map/all_to_all | solution.py:110
  72.6 3.7 %shard_map.46 = bf16[128,1024]{1,0:T(8,128)(2,1)S(1)} custom-call(s32[8]{0:T(128)S(1)} %get-tuple-element.34.slots, bf16[128,1024]{1,0:T(8,128)(2,1)S(1)} %get-tuple-element.13.query_ref, bf16[16,128,256]{2,1,0:T(8,128)(2,1)S(1)} %all-to-all-done.near_ref, bf16[16,128,256]{2,1,0:T(8,128)(2,1)S(1)} %all-to-all-done.1.far_ref), custom_call_target="tpu_custom_call" | custom-call | flops 536870912 | bytes 1048576 | tf_op jit(solution)/shard_map/pallas_call | solution.py:63
  76.3 1.9 %collective-permute-start.5 = (bf16[128,1024]{1,0:T(8,128)(2,1)S(1)}, bf16[128,1024]{1,0:T(8,128)(2,1)S(1)}, u32[]{:S(2)}, u32[]{:S(2)}) collective-permute-start(bf16[128,1024]{1,0:T(8,128)(2,1)S(1)} %shard_map.46), channel_id=1, source_target_pairs={{0,32},{1,33},{2,34},{3,35},{4,36},{5,37},{6,38},{7,39},{8,40},{9,... | collective-permute-start | bytes 786440 | tf_op jit(solution)/shard_map/ppermute | solution.py:134
  78.2 3.7 %shard_map.47 = bf16[128,1024]{1,0:T(8,128)(2,1)S(1)} custom-call(s32[8]{0:T(128)S(1)} %get-tuple-element.33.slots, bf16[128,1024]{1,0:T(8,128)(2,1)S(1)} %collective-permute-done.2.query_ref, bf16[16,128,256]{2,1,0:T(8,128)(2,1)S(1)} %all-to-all-done.near_ref, bf16[16,128,256]{2,1,0:T(8,128)(2,1)S(1)} %all-to-all-done.1.far_ref), custom_call_target="tpu_custom_call" | custom-call | flops 536870912 | bytes 1048576 | tf_op jit(solution)/shard_map/pallas_call | solution.py:63
  82.0 3.0 %collective-permute-start.6 = (bf16[128,1024]{1,0:T(8,128)(2,1)S(1)}, bf16[128,1024]{1,0:T(8,128)(2,1)S(1)}, u32[]{:S(2)}, u32[]{:S(2)}) collective-permute-start(bf16[128,1024]{1,0:T(8,128)(2,1)S(1)} %shard_map.47), channel_id=1, source_target_pairs={{0,44},{1,45},{2,46},{3,47},{4,32},{5,33},{6,34},{7,35},{8,36},{9,... | collective-permute-start | bytes 786440 | tf_op jit(solution)/shard_map/ppermute | solution.py:134
  85.0 3.7 %shard_map.48 = bf16[128,1024]{1,0:T(8,128)(2,1)S(1)} custom-call(s32[8]{0:T(128)S(1)} %get-tuple-element.32.slots, bf16[128,1024]{1,0:T(8,128)(2,1)S(1)} %collective-permute-done.3.query_ref, bf16[16,128,256]{2,1,0:T(8,128)(2,1)S(1)} %all-to-all-done.near_ref, bf16[16,128,256]{2,1,0:T(8,128)(2,1)S(1)} %all-to-all-done.1.far_ref), custom_call_target="tpu_custom_call" | custom-call | flops 536870912 | bytes 1048576 | tf_op jit(solution)/shard_map/pallas_call | solution.py:63
  88.7 2.8 %collective-permute-start.7 = (bf16[128,1024]{1,0:T(8,128)(2,1)S(1)}, bf16[128,1024]{1,0:T(8,128)(2,1)S(1)}, u32[]{:S(2)}, u32[]{:S(2)}) collective-permute-start(bf16[128,1024]{1,0:T(8,128)(2,1)S(1)} %shard_map.48), channel_id=1, source_target_pairs={{0,40},{1,41},{2,42},{3,43},{4,44},{5,45},{6,46},{7,47},{8,32},{9,... | collective-permute-start | bytes 786440 | tf_op jit(solution)/shard_map/ppermute | solution.py:134
  91.5 3.9 %shard_map.49 = bf16[128,1024]{1,0:T(8,128)(2,1)S(1)} custom-call(s32[8]{0:T(128)S(1)} %get-tuple-element.31.slots, bf16[128,1024]{1,0:T(8,128)(2,1)S(1)} %collective-permute-done.4.query_ref, bf16[16,128,256]{2,1,0:T(8,128)(2,1)S(1)} %all-to-all-done.near_ref, bf16[16,128,256]{2,1,0:T(8,128)(2,1)S(1)} %all-to-all-done.1.far_ref), custom_call_target="tpu_custom_call" | custom-call | flops 536870912 | bytes 1048576 | tf_op jit(solution)/shard_map/pallas_call | solution.py:63
  95.4 2.2 %collective-permute-start.8 = (bf16[128,1024]{1,0:T(8,128)(2,1)S(1)}, bf16[128,1024]{1,0:T(8,128)(2,1)S(1)}, u32[]{:S(2)}, u32[]{:S(2)}) collective-permute-start(bf16[128,1024]{1,0:T(8,128)(2,1)S(1)} %shard_map.49), channel_id=1, source_target_pairs={{0,36},{1,37},{2,38},{3,39},{4,40},{5,41},{6,42},{7,43},{8,44},{9,... | collective-permute-start | bytes 786440 | tf_op jit(solution)/shard_map/ppermute | solution.py:134
  97.7 0.0 collective-permute-done.5.refs_0_
  97.7 0.0 collective-permute-done.6.refs_1_
  97.7 7.9 %collective-permute-done.7.refs_2_ = bf16[128,1024]{1,0:T(8,128)(2,1)S(1)} collective-permute-done((bf16[128,1024]{1,0:T(8,128)(2,1)S(1)}, bf16[128,1024]{1,0:T(8,128)(2,1)S(1)}, u32[]{:S(2)}, u32[]{:S(2)}) %collective-permute-start.7) | collective-permute-done | bytes 262176 | tf_op jit(solution)/shard_map/ppermute | solution.py:134
  105.6 6.2 %collective-permute-done.8.refs_3_ = bf16[128,1024]{1,0:T(8,128)(2,1)S(1)} collective-permute-done((bf16[128,1024]{1,0:T(8,128)(2,1)S(1)}, bf16[128,1024]{1,0:T(8,128)(2,1)S(1)}, u32[]{:S(2)}, u32[]{:S(2)}) %collective-permute-start.8) | collective-permute-done | bytes 262176 | tf_op jit(solution)/shard_map/ppermute | solution.py:134
  111.8 1.6 %shard_map.50 = bf16[128,4096]{1,0:T(8,128)(2,1)} custom-call(s32[4]{0:T(128)S(1)} %and_select_fusion.2.heads, bf16[128,1024]{1,0:T(8,128)(2,1)S(1)} %collective-permute-done.5.refs_0_, bf16[128,1024]{1,0:T(8,128)(2,1)S(1)} %collective-permute-done.6.refs_1_, bf16[128,1024]{1,0:T(8,128)(2,1)S(1)} %collective-permute-done.7.refs_2_, ...), custom_call_target="tpu_custom_call" | custom-call | bytes 2097152 | tf_op jit(solution)/shard_map/pallas_call | solution.py:88
  (10 shorter events, 0.2 us)
Async XLA Ops:
  0.0 1.0 copy-start.1
  2.2 26.4 %copy-start = (bf16[1,128,4096]{2,1,0:T(8,128)(2,1)S(1)}, bf16[1,128,4096]{2,1,0:T(8,128)(2,1)}, u32[]{:S(2)}) copy-start(bf16[1,128,4096]{2,1,0:T(8,128)(2,1)} %param.4) | copy-start | bytes 3145732
  2.2 47.9 %all-to-all-start = ((bf16[16,128,256]{2,1,0:T(8,128)(2,1)}), bf16[16,128,256]{2,1,0:T(8,128)(2,1)S(1)}, u32[]{:S(2)}, u32[]{:S(2)}) async-start(bf16[16,128,256]{2,1,0:T(8,128)(2,1)} %bitcast.6), calls=%async_computation | async-start | bytes 2097152 | tf_op jit(solution)/shard_map/all_to_all | solution.py:110
  11.6 33.7 %collective-permute-start = (bf16[4,128,256]{2,1,0:T(8,128)(2,1)S(1)}, bf16[4,128,256]{2,1,0:T(8,128)(2,1)S(1)}, u32[]{:S(2)}, u32[]{:S(2)}) collective-permute-start(bf16[4,128,256]{2,1,0:T(8,128)(2,1)S(1)} %pad_maximum_fusion), channel_id=1, source_target_pairs={{0,16},{1,17},{2,18},{3,19},{4,20},{5,21},{6,22},{7,23},{8,24},{9,... | collective-permute-start | bytes 786440 | tf_op jit(solution)/shard_map/ppermute | solution.py:118
  29.5 10.9 %copy-start.2 = (s32[1,256,2]{1,2,0:T(2,128)S(1)}, s32[1,256,2]{1,2,0:T(2,128)}, u32[]{:S(2)}) copy-start(s32[1,256,2]{1,2,0:T(2,128)} %param.7) | copy-start | bytes 6148
  29.5 15.8 %collective-permute-start.4 = (bf16[128,1024]{1,0:T(8,128)(2,1)}, bf16[128,1024]{1,0:T(8,128)(2,1)S(1)}, u32[]{:S(2)}, u32[]{:S(2)}) collective-permute-start(bf16[128,1024]{1,0:T(8,128)(2,1)} %get-tuple-element.19), channel_id=1, source_target_pairs={{0,12},{1,13},{2,14},{3,15},{4,0},{5,1},{6,2},{7,3},{8,4},{9,5},{1... | collective-permute-start | bytes 786440 | tf_op jit(solution)/shard_map/ppermute | solution.py:124
  34.2 15.9 %collective-permute-start.2 = (bf16[128,1024]{1,0:T(8,128)(2,1)}, bf16[128,1024]{1,0:T(8,128)(2,1)S(1)}, u32[]{:S(2)}, u32[]{:S(2)}) collective-permute-start(bf16[128,1024]{1,0:T(8,128)(2,1)} %get-tuple-element.20), channel_id=1, source_target_pairs={{0,4},{1,5},{2,6},{3,7},{4,8},{5,9},{6,10},{7,11},{8,12},{9,13},{1... | collective-permute-start | bytes 786440 | tf_op jit(solution)/shard_map/ppermute | solution.py:124
  36.1 13.9 %collective-permute-start.3 = (bf16[128,1024]{1,0:T(8,128)(2,1)S(1)}, bf16[128,1024]{1,0:T(8,128)(2,1)S(1)}, u32[]{:S(2)}, u32[]{:S(2)}) collective-permute-start(bf16[128,1024]{1,0:T(8,128)(2,1)S(1)} %get-tuple-element.22), channel_id=1, source_target_pairs={{0,8},{1,9},{2,10},{3,11},{4,12},{5,13},{6,14},{7,15},{8,0},{9,1},... | collective-permute-start | bytes 786440 | tf_op jit(solution)/shard_map/ppermute | solution.py:124
  40.5 4.8 %collective-permute-start.1 = (s32[32,8]{1,0:T(8,128)S(1)}, s32[32,8]{1,0:T(8,128)S(1)}, u32[]{:S(2)}, u32[]{:S(2)}) collective-permute-start(s32[32,8]{1,0:T(8,128)S(1)} %reshape_squeeze.3), channel_id=1, source_target_pairs={{0,480},{1,481},{2,482},{3,483},{4,484},{5,485},{6,486},{7,487},{8... | collective-permute-start | bytes 3080 | tf_op jit(solution)/shard_map/ppermute | solution.py:120
  51.1 21.5 %all-to-all-start.1 = ((bf16[16,128,256]{2,1,0:T(8,128)(2,1)}), bf16[16,128,256]{2,1,0:T(8,128)(2,1)S(1)}, u32[]{:S(2)}, u32[]{:S(2)}) async-start(bf16[16,128,256]{2,1,0:T(8,128)(2,1)} %bitcast.35), calls=%async_computation.1 | async-start | bytes 2097152 | tf_op jit(solution)/shard_map/all_to_all | solution.py:110
  76.3 21.4 %collective-permute-start.5 = (bf16[128,1024]{1,0:T(8,128)(2,1)S(1)}, bf16[128,1024]{1,0:T(8,128)(2,1)S(1)}, u32[]{:S(2)}, u32[]{:S(2)}) collective-permute-start(bf16[128,1024]{1,0:T(8,128)(2,1)S(1)} %shard_map.46), channel_id=1, source_target_pairs={{0,32},{1,33},{2,34},{3,35},{4,36},{5,37},{6,38},{7,39},{8,40},{9,... | collective-permute-start | bytes 786440 | tf_op jit(solution)/shard_map/ppermute | solution.py:134
  82.0 15.7 %collective-permute-start.6 = (bf16[128,1024]{1,0:T(8,128)(2,1)S(1)}, bf16[128,1024]{1,0:T(8,128)(2,1)S(1)}, u32[]{:S(2)}, u32[]{:S(2)}) collective-permute-start(bf16[128,1024]{1,0:T(8,128)(2,1)S(1)} %shard_map.47), channel_id=1, source_target_pairs={{0,44},{1,45},{2,46},{3,47},{4,32},{5,33},{6,34},{7,35},{8,36},{9,... | collective-permute-start | bytes 786440 | tf_op jit(solution)/shard_map/ppermute | solution.py:134
  88.7 16.9 %collective-permute-start.7 = (bf16[128,1024]{1,0:T(8,128)(2,1)S(1)}, bf16[128,1024]{1,0:T(8,128)(2,1)S(1)}, u32[]{:S(2)}, u32[]{:S(2)}) collective-permute-start(bf16[128,1024]{1,0:T(8,128)(2,1)S(1)} %shard_map.48), channel_id=1, source_target_pairs={{0,40},{1,41},{2,42},{3,43},{4,44},{5,45},{6,46},{7,47},{8,32},{9,... | collective-permute-start | bytes 786440 | tf_op jit(solution)/shard_map/ppermute | solution.py:134
  95.4 16.4 %collective-permute-start.8 = (bf16[128,1024]{1,0:T(8,128)(2,1)S(1)}, bf16[128,1024]{1,0:T(8,128)(2,1)S(1)}, u32[]{:S(2)}, u32[]{:S(2)}) collective-permute-start(bf16[128,1024]{1,0:T(8,128)(2,1)S(1)} %shard_map.49), channel_id=1, source_target_pairs={{0,36},{1,37},{2,38},{3,39},{4,40},{5,41},{6,42},{7,43},{8,44},{9,... | collective-permute-start | bytes 786440 | tf_op jit(solution)/shard_map/ppermute | solution.py:134

commit v3 on v2

v3 whole, which is shorter than its diff:
```python
import math

import jax
import jax.numpy as jnp
from jax import lax
from jax.experimental import pallas as pl
from jax.experimental.pallas import tpu as pltpu
from jax.sharding import PartitionSpec as P

TILE = 128
HEADS = 4
GROUP = 8
HEAD_SIZE = 128
PICKS = 8
WIDE = GROUP * HEAD_SIZE
SECTIONS = 16
SIDE = 4
PLANE = SIDE * SIDE
TILES = 2 * PLANE
AXES = ("pipe", "dp")
SCALE = math.log2(math.e) / math.sqrt(HEAD_SIZE)
VMEM = pl.BlockSpec(memory_space=pltpu.VMEM)
SMEM = pl.BlockSpec(memory_space=pltpu.SMEM)


def route(step, swap, turn):
    pairs = []
    for section in range(SECTIONS):
        for tile in range(TILES):
            half, row, column = tile // PLANE, tile // SIDE % SIDE, tile % SIDE
            target = (half ^ swap) * PLANE + (row + turn) % SIDE * SIDE + column
            pairs.append((section * TILES + tile, (section + step) % SECTIONS * TILES + target))
    return pairs


def attention_kernel(slots, *refs):
    query_refs, near_ref, far_ref = refs[:SIDE], refs[SIDE], refs[SIDE + 1]
    out_refs, k_sel, v_sel = refs[SIDE + 2 : 2 * SIDE + 2], refs[-2], refs[-1]
    for turn in range(SIDE):
        attend(slots, turn, query_refs[turn], near_ref, far_ref, out_refs[turn], k_sel, v_sel)


def attend(slots, turn, query_ref, near_ref, far_ref, out_ref, k_sel, v_sel):
    for pick in range(PICKS):
        slot = slots[turn, pick]
        rows = pl.ds(pick * TILE, TILE)
        for side, held in enumerate((near_ref, far_ref)):

            @pl.when(slot // PLANE == side)
            def _():
                k_sel[rows, :] = held[slot % PLANE, :, :HEAD_SIZE]
                v_sel[rows, :HEAD_SIZE] = held[slot % PLANE, :, HEAD_SIZE:]

    v_sel[:, HEAD_SIZE:] = jnp.ones((PICKS * TILE, HEAD_SIZE), jnp.bfloat16)

    def scores_of(head):
        return lax.dot_general(
            query_ref[:, pl.ds(head * HEAD_SIZE, HEAD_SIZE)], k_sel[...], (((1,), (1,)), ((), ())),
            preferred_element_type=jnp.float32,
        )

    later = scores_of(0)
    for head in range(GROUP):
        scores = later
        if head + 1 < GROUP:
            later = scores_of(head + 1)
        largest = jnp.max(scores, axis=-1, keepdims=True)
        weights = jnp.exp2((scores - largest) * SCALE).astype(jnp.bfloat16)
        mixed = jnp.dot(weights, v_sel[...], preferred_element_type=jnp.float32)
        out_ref[:, pl.ds(head * HEAD_SIZE, HEAD_SIZE)] = (
            mixed[:, :HEAD_SIZE] / mixed[:, HEAD_SIZE:]
        ).astype(jnp.bfloat16)


def attention(slots, queries, near, far):
    return pl.pallas_call(
        attention_kernel,
        out_shape=[jax.ShapeDtypeStruct((TILE, WIDE), jnp.bfloat16)] * SIDE,
        in_specs=[SMEM] + [VMEM] * (SIDE + 2),
        out_specs=[VMEM] * SIDE,
        scratch_shapes=[
            pltpu.VMEM((PICKS * TILE, HEAD_SIZE), jnp.bfloat16),
            pltpu.VMEM((PICKS * TILE, 2 * HEAD_SIZE), jnp.bfloat16),
        ],
        compiler_params=pltpu.CompilerParams(vmem_limit_bytes=24 * 1024 * 1024),
        cost_estimate=pl.CostEstimate(
            flops=2 * 2 * SIDE * GROUP * TILE * PICKS * TILE * HEAD_SIZE,
            bytes_accessed=4 * 1024 * 1024,
            transcendentals=SIDE * GROUP * TILE * PICKS * TILE,
        ),
    )(slots, *queries, near, far)


def assemble_kernel(heads, *refs):
    pieces, out_ref, sems = refs[:SIDE], refs[SIDE], refs[SIDE + 1]
    copies = []
    for turn in range(SIDE):
        columns = pl.ds(pl.multiple_of(heads[turn] * WIDE, WIDE), WIDE)
        copies.append(pltpu.make_async_copy(pieces[turn], out_ref.at[:, columns], sems.at[turn]))
        copies[-1].start()
    for copy in copies:
        copy.wait()


def assemble(heads, pieces):
    return pl.pallas_call(
        assemble_kernel,
        out_shape=jax.ShapeDtypeStruct((TILE, HEADS * WIDE), jnp.bfloat16),
        in_specs=[SMEM] + [VMEM] * SIDE,
        out_specs=pl.BlockSpec(memory_space=pl.ANY),
        scratch_shapes=[pltpu.SemaphoreType.DMA((SIDE,))],
        compiler_params=pltpu.CompilerParams(vmem_limit_bytes=6 * 1024 * 1024),
        cost_estimate=pl.CostEstimate(flops=0, bytes_accessed=2 * 1024 * 1024, transcendentals=0),
    )(heads, *pieces)


def repeat_kernel(held_ref, sent_ref, sems):
    copies = []
    for slot in range(PLANE):
        copies.append(
            pltpu.make_async_copy(held_ref.at[slot // SIDE], sent_ref.at[slot], sems.at[slot])
        )
        copies[-1].start()
    for copy in copies:
        copy.wait()


def repeated(held, cost):
    return pl.pallas_call(
        repeat_kernel,
        out_shape=jax.ShapeDtypeStruct((PLANE,) + held.shape[1:], held.dtype),
        in_specs=[VMEM],
        out_specs=pl.BlockSpec(memory_space=pl.ANY),
        scratch_shapes=[pltpu.SemaphoreType.DMA((PLANE,))],
        compiler_params=pltpu.CompilerParams(vmem_limit_bytes=6 * 1024 * 1024),
        cost_estimate=pl.CostEstimate(flops=cost, bytes_accessed=1280 * 1024, transcendentals=0),
    )(held)


def on_device(queries, keys, values, block_pairs):
    queries, keys, values = queries[0], keys[0], values[0]
    place = lax.axis_index("dp")
    half, row, column = place // PLANE, place // SIDE % SIDE, place % SIDE
    groups = [[h * PLANE + i for i in range(PLANE)] for h in range(2)]

    def head_columns(array, head):
        return array[:, head * HEAD_SIZE : (head + 1) * HEAD_SIZE]

    def spread(sent):
        return lax.all_to_all(sent, "dp", 0, 0, axis_index_groups=groups)

    kv = jnp.stack(
        [
            jnp.concatenate([head_columns(keys, h), head_columns(values, h)], axis=1)
            for h in range(HEADS)
        ]
    )
    far = lax.ppermute(kv, AXES, route(0, 1, 0))
    near_landed = spread(repeated(kv, 0))
    pairs = lax.ppermute(block_pairs[0, :, 1].reshape(TILES, PICKS), AXES, route(-1, 0, 0))
    heads = (row + jnp.arange(SIDE, dtype=jnp.int32)) % SIDE
    pieces = [lax.dynamic_slice_in_dim(queries, heads[turn] * WIDE, WIDE, 1) for turn in range(SIDE)]
    for turn in range(1, SIDE):
        pieces[turn] = lax.ppermute(pieces[turn], AXES, route(0, 0, turn))
    far_sent = repeated(far, 2 * 10**10)
    far_sent, near_landed, pairs, *pieces = lax.optimization_barrier(
        (far_sent, near_landed, pairs, *pieces)
    )
    far_landed = spread(far_sent)

    blocks = half * PLANE + (row - jnp.arange(SIDE, dtype=jnp.int32)) % SIDE * SIDE + column
    chosen = jnp.take(pairs, blocks, axis=0)
    slots = (chosen % PLANE) + ((chosen // PLANE) ^ half) * PLANE
    mixed = attention(slots, pieces, near_landed, far_landed)
    back = [lax.ppermute(mixed[turn], AXES, route(1, 0, -turn)) for turn in range(SIDE)]
    return assemble(heads, back)[None]


def solution(mesh):
    placed = (
        P("pipe", "dp", None),
        P("pipe", "dp", None),
        P("pipe", "dp", None),
        P("pipe", None, None),
    )
    return jax.shard_map(
        on_device, mesh=mesh, in_specs=placed, out_specs=P("pipe", "dp", None), check_vma=False
    )
```

time: 115 us -> 110 us (0.957)
  starting transfers between devices: 52.3 us -> 58.7 us
  Pallas kernels: 16.6 us -> 11.7 us
  waiting for transfers between devices: 36.2 us -> 31.4 us
  local copies, waits for them, and re-layouts: 5.33 us -> 3.59 us
    pallas_call x4 -> x3, Pallas kernels: 15 us -> 10.1 us  [the longest x1 7.91 us: attention(): pl.pallas_call(attention_kernel, out_shape=[jax.ShapeDtypeStruct((TILE, W...]
    all_to_all x2, waiting for transfers between devices: 15.9 us -> 12.3 us  [spread(): return lax.all_to_all(sent, 'dp', 0, 0, axis_index_groups=groups)]
    ppermute x4, starting transfers between devices: 9.97 us -> 13 us  [on_device(): lax.ppermute(mixed[turn], AXES, route(1, 0, -turn))]
    broadcast_in_dim x2 -> x0, local copies, waits for them, and re-layouts: 2.15 us -> none  [spread(): sent = jnp.broadcast_to(held[:, None], (HEADS, SIDE) + held.shape[1:])]
    ppermute x1, starting transfers between devices: 13.8 us -> 15.7 us  [on_device(): far = lax.ppermute(kv, AXES, route(0, 1, 0))]
    ppermute x1, waiting for transfers between devices: 1.42 us -> 0.01 us  [on_device(): lax.ppermute(block_pairs[0, :, 1].reshape(TILES, PICKS), AXES, route(-1,...]
  transfers between devices with their start and end apart: 11 -> 11, of which waited for: 5 -> 8; matrix products, arithmetic and copies ran while one was open for 2% -> 3% of each run, Pallas kernels for 10% -> 2%
where the time goes in v3:
time: 110 us; the launch traced here: 108 us
  starting transfers between devices  58.7 us (53%)
  waiting for transfers between devices  31.4 us (29%)
  Pallas kernels  11.7 us (11%)
  local copies, waits for them, and re-layouts  3.59 us (3%)
  between operations  2.8 us (3%)
    ppermute x1, starting transfers between devices, on_device(): far = lax.ppermute(kv, AXES, route(0, 1, 0))  15.7 us
    all_to_all x2, starting transfers between devices, spread(): return lax.all_to_all(sent, 'dp', 0, 0, axis_index_groups=groups)  14.4 us
    ppermute x4, waiting for transfers between devices, on_device(): lax.ppermute(mixed[turn], AXES, route(1, 0, -turn))  13.7 us
    ppermute x4, starting transfers between devices, on_device(): lax.ppermute(mixed[turn], AXES, route(1, 0, -turn))  13 us
    all_to_all x2, waiting for transfers between devices, spread(): return lax.all_to_all(sent, 'dp', 0, 0, axis_index_groups=groups)  12.3 us
    ppermute x3, starting transfers between devices, on_device(): pieces[turn] = lax.ppermute(pieces[turn], AXES, route(0, 0, turn))  11.3 us
    pallas_call x1, Pallas kernels, attention(): pl.pallas_call(attention_kernel, out_shape=[jax.ShapeDtypeStruct((TILE, W...  7.91 us
    ppermute x3, waiting for transfers between devices, on_device(): pieces[turn] = lax.ppermute(pieces[turn], AXES, route(0, 0, turn))  5.36 us
  transfers between devices with their start and end apart: 11, of which 8 were waited for; matrix products, arithmetic and copies ran while one was open for 3% of the time, Pallas kernels for 2%

profile of v3, /device:TPU:6, one launch (start us, length us, event | category | flops | bytes accessed | tf_op | source)
XLA Modules:
  0.0 108.4 jit_solution(3556484920792728836)
XLA Ops:
  0.0 0.0 copy-start
  0.0 0.9 fusion.16
  0.9 0.1 copy-done
  1.1 15.7 %collective-permute-start = (bf16[4,128,256]{2,1,0:T(8,128)(2,1)S(1)}, bf16[4,128,256]{2,1,0:T(8,128)(2,1)S(1)}, u32[]{:S(2)}, u32[]{:S(2)}) collective-permute-start(bf16[4,128,256]{2,1,0:T(8,128)(2,1)S(1)} %pad_maximum_fusion.held_ref), channel_id=1, source_target_pairs={{0,16},{1,17},{2,18},{3,19},{4,20},{5,21},{6,22},{7,23},{8,24},{9,... | collective-permute-start | bytes 786440 | tf_op jit(solution)/shard_map/ppermute | solution.py:158
  16.8 1.1 %shard_map.47 = bf16[16,128,256]{2,1,0:T(8,128)(2,1)} custom-call(bf16[4,128,256]{2,1,0:T(8,128)(2,1)S(1)} %pad_maximum_fusion.held_ref), custom_call_target="tpu_custom_call" | custom-call | bytes 1310720 | tf_op jit(solution)/shard_map/pallas_call | solution.py:129
  17.9 0.0 copy-start.1
  17.9 7.4 %all-to-all-start = ((bf16[16,128,256]{2,1,0:T(8,128)(2,1)}), bf16[16,128,256]{2,1,0:T(8,128)(2,1)S(1)}, u32[]{:S(2)}, u32[]{:S(2)}) async-start(bf16[16,128,256]{2,1,0:T(8,128)(2,1)} %shard_map.47), calls=%async_computation | async-start | bytes 2097152 | tf_op jit(solution)/shard_map/all_to_all | solution.py:150
  25.4 0.0 copy-done.1
  25.4 0.1 reshape_squeeze.3
  25.5 4.3 %collective-permute-start.1 = (s32[32,8]{1,0:T(8,128)S(1)}, s32[32,8]{1,0:T(8,128)S(1)}, u32[]{:S(2)}, u32[]{:S(2)}) collective-permute-start(s32[32,8]{1,0:T(8,128)S(1)} %reshape_squeeze.3), channel_id=1, source_target_pairs={{0,480},{1,481},{2,482},{3,483},{4,484},{5,485},{6,486},{7,487},{8... | collective-permute-start | bytes 3080 | tf_op jit(solution)/shard_map/ppermute | solution.py:160
  29.8 0.7 fusion.17
  33.0 1.3 %dynamic-slice_bitcast_fusion = (bf16[128,1024]{1,0:T(8,128)(2,1)S(1)}, bf16[128,1024]{1,0:T(8,128)(2,1)S(1)}, bf16[128,1024]{1,0:T(8,128)(2,1)S(1)}, bf16[128,1024]{1,0:T(8,128)(2,1)S(1)}) fusion(bf16[1,128,4096]{2,1,0:T(8,128)(2,1)} %param.4, s32[]{:T(128)S(6)} %select_n.92, s32[]{:T(128)S(6)} %select_n.90, s32[]{:T(128)S(6)} %select_n.89, s32[]{:T(128)S(6)} %select_n.91), kind=kLoop, calls=%fused_computation.2 | loop fusion | bytes 2097168 | tf_op jit(solution)/shard_map/dynamic_slice | solution.py:162
  34.3 3.4 %collective-permute-start.2 = (bf16[128,1024]{1,0:T(8,128)(2,1)S(1)}, bf16[128,1024]{1,0:T(8,128)(2,1)S(1)}, u32[]{:S(2)}, u32[]{:S(2)}) collective-permute-start(bf16[128,1024]{1,0:T(8,128)(2,1)S(1)} %get-tuple-element.28), channel_id=1, source_target_pairs={{0,4},{1,5},{2,6},{3,7},{4,8},{5,9},{6,10},{7,11},{8,12},{9,13},{1... | collective-permute-start | bytes 786440 | tf_op jit(solution)/shard_map/ppermute | solution.py:164
  37.7 4.6 %collective-permute-start.3 = (bf16[128,1024]{1,0:T(8,128)(2,1)S(1)}, bf16[128,1024]{1,0:T(8,128)(2,1)S(1)}, u32[]{:S(2)}, u32[]{:S(2)}) collective-permute-start(bf16[128,1024]{1,0:T(8,128)(2,1)S(1)} %get-tuple-element.30), channel_id=1, source_target_pairs={{0,8},{1,9},{2,10},{3,11},{4,12},{5,13},{6,14},{7,15},{8,0},{9,1},... | collective-permute-start | bytes 786440 | tf_op jit(solution)/shard_map/ppermute | solution.py:164
  42.3 3.4 %collective-permute-start.4 = (bf16[128,1024]{1,0:T(8,128)(2,1)S(1)}, bf16[128,1024]{1,0:T(8,128)(2,1)S(1)}, u32[]{:S(2)}, u32[]{:S(2)}) collective-permute-start(bf16[128,1024]{1,0:T(8,128)(2,1)S(1)} %get-tuple-element.27), channel_id=1, source_target_pairs={{0,12},{1,13},{2,14},{3,15},{4,0},{5,1},{6,2},{7,3},{8,4},{9,5},{1... | collective-permute-start | bytes 786440 | tf_op jit(solution)/shard_map/ppermute | solution.py:164
  45.7 0.0 collective-permute-done.held_ref
  45.7 1.1 %shard_map.46 = bf16[16,128,256]{2,1,0:T(8,128)(2,1)} custom-call(bf16[4,128,256]{2,1,0:T(8,128)(2,1)S(1)} %collective-permute-done.held_ref), custom_call_target="tpu_custom_call" | custom-call | flops 20000000000 | bytes 1310720 | tf_op jit(solution)/shard_map/pallas_call | solution.py:129
  46.8 0.0 collective-permute-done.1
  46.8 0.2 collective-permute-done.2.refs_1_
  47.0 3.9 %collective-permute-done.3.refs_2_ = bf16[128,1024]{1,0:T(8,128)(2,1)S(1)} collective-permute-done((bf16[128,1024]{1,0:T(8,128)(2,1)S(1)}, bf16[128,1024]{1,0:T(8,128)(2,1)S(1)}, u32[]{:S(2)}, u32[]{:S(2)}) %collective-permute-start.3) | collective-permute-done | bytes 262176 | tf_op jit(solution)/shard_map/ppermute | solution.py:164
  50.9 1.3 %collective-permute-done.4.refs_3_ = bf16[128,1024]{1,0:T(8,128)(2,1)S(1)} collective-permute-done((bf16[128,1024]{1,0:T(8,128)(2,1)S(1)}, bf16[128,1024]{1,0:T(8,128)(2,1)S(1)}, u32[]{:S(2)}, u32[]{:S(2)}) %collective-permute-start.4) | collective-permute-done | bytes 262176 | tf_op jit(solution)/shard_map/ppermute | solution.py:164
  52.2 0.0 all-to-all-done.refs_4_
  52.2 7.0 %all-to-all-start.1 = ((bf16[16,128,256]{2,1,0:T(8,128)(2,1)}), bf16[16,128,256]{2,1,0:T(8,128)(2,1)S(1)}, u32[]{:S(2)}, u32[]{:S(2)}) async-start(bf16[16,128,256]{2,1,0:T(8,128)(2,1)} %shard_map.46), calls=%async_computation.1 | async-start | bytes 2097152 | tf_op jit(solution)/shard_map/all_to_all | solution.py:150
  59.2 0.6 gather_fusion
  59.8 0.1 fusion.slots
  59.8 12.3 %all-to-all-done.1.refs_5_ = bf16[16,128,256]{2,1,0:T(8,128)(2,1)S(1)} async-done(((bf16[16,128,256]{2,1,0:T(8,128)(2,1)}), bf16[16,128,256]{2,1,0:T(8,128)(2,1)S(1)}, u32[]{:S(2)}, u32[]{:S(2)}) %all-to-all-start.1) | async-done | bytes 1048608 | tf_op jit(solution)/shard_map/all_to_all | solution.py:150
  72.2 7.9 %shard_map.48 = (bf16[128,1024]{1,0:T(8,128)(2,1)S(1)}, bf16[128,1024]{1,0:T(8,128)(2,1)S(1)}, bf16[128,1024]{1,0:T(8,128)(2,1)S(1)}, bf16[128,1024]{1,0:T(8,128)(2,1)S(1)}) custom-call(s32[4,8]{1,0:T(4,128)S(1)} %fusion.slots, bf16[128,1024]{1,0:T(8,128)(2,1)S(1)} %get-tuple-element.17.refs_0_, bf16[128,1024]{1,0:T(8,128)(2,1)S(1)} %collective-permute-done.2.refs_1_, ...), custom_call_target="tpu_custom_call" | custom-call | flops 2147483648 | bytes 4194304 | tf_op jit(solution)/shard_map/pallas_call | solution.py:76
  80.1 1.9 %collective-permute-start.5 = (bf16[128,1024]{1,0:T(8,128)(2,1)S(1)}, bf16[128,1024]{1,0:T(8,128)(2,1)S(1)}, u32[]{:S(2)}, u32[]{:S(2)}) collective-permute-start(bf16[128,1024]{1,0:T(8,128)(2,1)S(1)} %get-tuple-element.23), channel_id=1, source_target_pairs={{0,32},{1,33},{2,34},{3,35},{4,36},{5,37},{6,38},{7,39},{8,40},{9,... | collective-permute-start | bytes 786440 | tf_op jit(solution)/shard_map/ppermute | solution.py:175
  82.0 5.3 %collective-permute-start.6 = (bf16[128,1024]{1,0:T(8,128)(2,1)S(1)}, bf16[128,1024]{1,0:T(8,128)(2,1)S(1)}, u32[]{:S(2)}, u32[]{:S(2)}) collective-permute-start(bf16[128,1024]{1,0:T(8,128)(2,1)S(1)} %get-tuple-element.24), channel_id=1, source_target_pairs={{0,44},{1,45},{2,46},{3,47},{4,32},{5,33},{6,34},{7,35},{8,36},{9,... | collective-permute-start | bytes 786440 | tf_op jit(solution)/shard_map/ppermute | solution.py:175
  87.3 3.0 %collective-permute-start.7 = (bf16[128,1024]{1,0:T(8,128)(2,1)S(1)}, bf16[128,1024]{1,0:T(8,128)(2,1)S(1)}, u32[]{:S(2)}, u32[]{:S(2)}) collective-permute-start(bf16[128,1024]{1,0:T(8,128)(2,1)S(1)} %get-tuple-element.25), channel_id=1, source_target_pairs={{0,40},{1,41},{2,42},{3,43},{4,44},{5,45},{6,46},{7,47},{8,32},{9,... | collective-permute-start | bytes 786440 | tf_op jit(solution)/shard_map/ppermute | solution.py:175
  90.4 2.8 %collective-permute-start.8 = (bf16[128,1024]{1,0:T(8,128)(2,1)S(1)}, bf16[128,1024]{1,0:T(8,128)(2,1)S(1)}, u32[]{:S(2)}, u32[]{:S(2)}) collective-permute-start(bf16[128,1024]{1,0:T(8,128)(2,1)S(1)} %get-tuple-element.26), channel_id=1, source_target_pairs={{0,36},{1,37},{2,38},{3,39},{4,40},{5,41},{6,42},{7,43},{8,44},{9,... | collective-permute-start | bytes 786440 | tf_op jit(solution)/shard_map/ppermute | solution.py:175
  93.1 1.3 %collective-permute-done.5.refs_0_ = bf16[128,1024]{1,0:T(8,128)(2,1)S(1)} collective-permute-done((bf16[128,1024]{1,0:T(8,128)(2,1)S(1)}, bf16[128,1024]{1,0:T(8,128)(2,1)S(1)}, u32[]{:S(2)}, u32[]{:S(2)}) %collective-permute-start.5) | collective-permute-done | bytes 262176 | tf_op jit(solution)/shard_map/ppermute | solution.py:175
  94.4 3.5 %collective-permute-done.6.refs_1_ = bf16[128,1024]{1,0:T(8,128)(2,1)S(1)} collective-permute-done((bf16[128,1024]{1,0:T(8,128)(2,1)S(1)}, bf16[128,1024]{1,0:T(8,128)(2,1)S(1)}, u32[]{:S(2)}, u32[]{:S(2)}) %collective-permute-start.6) | collective-permute-done | bytes 262176 | tf_op jit(solution)/shard_map/ppermute | solution.py:175
  97.9 6.2 %collective-permute-done.7.refs_2_ = bf16[128,1024]{1,0:T(8,128)(2,1)S(1)} collective-permute-done((bf16[128,1024]{1,0:T(8,128)(2,1)S(1)}, bf16[128,1024]{1,0:T(8,128)(2,1)S(1)}, u32[]{:S(2)}, u32[]{:S(2)}) %collective-permute-start.7) | collective-permute-done | bytes 262176 | tf_op jit(solution)/shard_map/ppermute | solution.py:175
  104.1 2.8 %collective-permute-done.8.refs_3_ = bf16[128,1024]{1,0:T(8,128)(2,1)S(1)} collective-permute-done((bf16[128,1024]{1,0:T(8,128)(2,1)S(1)}, bf16[128,1024]{1,0:T(8,128)(2,1)S(1)}, u32[]{:S(2)}, u32[]{:S(2)}) %collective-permute-start.8) | collective-permute-done | bytes 262176 | tf_op jit(solution)/shard_map/ppermute | solution.py:175
  106.8 1.5 %shard_map.49 = bf16[128,4096]{1,0:T(8,128)(2,1)} custom-call(s32[4]{0:T(128)S(1)} %and_select_fusion.2.heads, bf16[128,1024]{1,0:T(8,128)(2,1)S(1)} %collective-permute-done.5.refs_0_, bf16[128,1024]{1,0:T(8,128)(2,1)S(1)} %collective-permute-done.6.refs_1_, bf16[128,1024]{1,0:T(8,128)(2,1)S(1)} %collective-permute-done.7.refs_2_, ...), custom_call_target="tpu_custom_call" | custom-call | bytes 2097152 | tf_op jit(solution)/shard_map/pallas_call | solution.py:106
  (9 shorter events, 0.2 us)
Async XLA Ops:
  0.0 1.0 copy-start
  1.1 44.6 %collective-permute-start = (bf16[4,128,256]{2,1,0:T(8,128)(2,1)S(1)}, bf16[4,128,256]{2,1,0:T(8,128)(2,1)S(1)}, u32[]{:S(2)}, u32[]{:S(2)}) collective-permute-start(bf16[4,128,256]{2,1,0:T(8,128)(2,1)S(1)} %pad_maximum_fusion.held_ref), channel_id=1, source_target_pairs={{0,16},{1,17},{2,18},{3,19},{4,20},{5,21},{6,22},{7,23},{8,24},{9,... | collective-permute-start | bytes 786440 | tf_op jit(solution)/shard_map/ppermute | solution.py:158
  17.9 7.4 %copy-start.1 = (s32[1,256,2]{1,2,0:T(2,128)S(1)}, s32[1,256,2]{1,2,0:T(2,128)}, u32[]{:S(2)}) copy-start(s32[1,256,2]{1,2,0:T(2,128)} %param.7) | copy-start | bytes 6148
  17.9 34.2 %all-to-all-start = ((bf16[16,128,256]{2,1,0:T(8,128)(2,1)}), bf16[16,128,256]{2,1,0:T(8,128)(2,1)S(1)}, u32[]{:S(2)}, u32[]{:S(2)}) async-start(bf16[16,128,256]{2,1,0:T(8,128)(2,1)} %shard_map.47), calls=%async_computation | async-start | bytes 2097152 | tf_op jit(solution)/shard_map/all_to_all | solution.py:150
  25.5 21.3 %collective-permute-start.1 = (s32[32,8]{1,0:T(8,128)S(1)}, s32[32,8]{1,0:T(8,128)S(1)}, u32[]{:S(2)}, u32[]{:S(2)}) collective-permute-start(s32[32,8]{1,0:T(8,128)S(1)} %reshape_squeeze.3), channel_id=1, source_target_pairs={{0,480},{1,481},{2,482},{3,483},{4,484},{5,485},{6,486},{7,487},{8... | collective-permute-start | bytes 3080 | tf_op jit(solution)/shard_map/ppermute | solution.py:160
  34.3 12.7 %collective-permute-start.2 = (bf16[128,1024]{1,0:T(8,128)(2,1)S(1)}, bf16[128,1024]{1,0:T(8,128)(2,1)S(1)}, u32[]{:S(2)}, u32[]{:S(2)}) collective-permute-start(bf16[128,1024]{1,0:T(8,128)(2,1)S(1)} %get-tuple-element.28), channel_id=1, source_target_pairs={{0,4},{1,5},{2,6},{3,7},{4,8},{5,9},{6,10},{7,11},{8,12},{9,13},{1... | collective-permute-start | bytes 786440 | tf_op jit(solution)/shard_map/ppermute | solution.py:164
  37.7 13.2 %collective-permute-start.3 = (bf16[128,1024]{1,0:T(8,128)(2,1)S(1)}, bf16[128,1024]{1,0:T(8,128)(2,1)S(1)}, u32[]{:S(2)}, u32[]{:S(2)}) collective-permute-start(bf16[128,1024]{1,0:T(8,128)(2,1)S(1)} %get-tuple-element.30), channel_id=1, source_target_pairs={{0,8},{1,9},{2,10},{3,11},{4,12},{5,13},{6,14},{7,15},{8,0},{9,1},... | collective-permute-start | bytes 786440 | tf_op jit(solution)/shard_map/ppermute | solution.py:164
  42.3 9.9 %collective-permute-start.4 = (bf16[128,1024]{1,0:T(8,128)(2,1)S(1)}, bf16[128,1024]{1,0:T(8,128)(2,1)S(1)}, u32[]{:S(2)}, u32[]{:S(2)}) collective-permute-start(bf16[128,1024]{1,0:T(8,128)(2,1)S(1)} %get-tuple-element.27), channel_id=1, source_target_pairs={{0,12},{1,13},{2,14},{3,15},{4,0},{5,1},{6,2},{7,3},{8,4},{9,5},{1... | collective-permute-start | bytes 786440 | tf_op jit(solution)/shard_map/ppermute | solution.py:164
  52.2 20.0 %all-to-all-start.1 = ((bf16[16,128,256]{2,1,0:T(8,128)(2,1)}), bf16[16,128,256]{2,1,0:T(8,128)(2,1)S(1)}, u32[]{:S(2)}, u32[]{:S(2)}) async-start(bf16[16,128,256]{2,1,0:T(8,128)(2,1)} %shard_map.46), calls=%async_computation.1 | async-start | bytes 2097152 | tf_op jit(solution)/shard_map/all_to_all | solution.py:150
  80.1 14.3 %collective-permute-start.5 = (bf16[128,1024]{1,0:T(8,128)(2,1)S(1)}, bf16[128,1024]{1,0:T(8,128)(2,1)S(1)}, u32[]{:S(2)}, u32[]{:S(2)}) collective-permute-start(bf16[128,1024]{1,0:T(8,128)(2,1)S(1)} %get-tuple-element.23), channel_id=1, source_target_pairs={{0,32},{1,33},{2,34},{3,35},{4,36},{5,37},{6,38},{7,39},{8,40},{9,... | collective-permute-start | bytes 786440 | tf_op jit(solution)/shard_map/ppermute | solution.py:175
  82.0 15.9 %collective-permute-start.6 = (bf16[128,1024]{1,0:T(8,128)(2,1)S(1)}, bf16[128,1024]{1,0:T(8,128)(2,1)S(1)}, u32[]{:S(2)}, u32[]{:S(2)}) collective-permute-start(bf16[128,1024]{1,0:T(8,128)(2,1)S(1)} %get-tuple-element.24), channel_id=1, source_target_pairs={{0,44},{1,45},{2,46},{3,47},{4,32},{5,33},{6,34},{7,35},{8,36},{9,... | collective-permute-start | bytes 786440 | tf_op jit(solution)/shard_map/ppermute | solution.py:175
  87.3 16.7 %collective-permute-start.7 = (bf16[128,1024]{1,0:T(8,128)(2,1)S(1)}, bf16[128,1024]{1,0:T(8,128)(2,1)S(1)}, u32[]{:S(2)}, u32[]{:S(2)}) collective-permute-start(bf16[128,1024]{1,0:T(8,128)(2,1)S(1)} %get-tuple-element.25), channel_id=1, source_target_pairs={{0,40},{1,41},{2,42},{3,43},{4,44},{5,45},{6,46},{7,47},{8,32},{9,... | collective-permute-start | bytes 786440 | tf_op jit(solution)/shard_map/ppermute | solution.py:175
  90.4 16.5 %collective-permute-start.8 = (bf16[128,1024]{1,0:T(8,128)(2,1)S(1)}, bf16[128,1024]{1,0:T(8,128)(2,1)S(1)}, u32[]{:S(2)}, u32[]{:S(2)}) collective-permute-start(bf16[128,1024]{1,0:T(8,128)(2,1)S(1)} %get-tuple-element.26), channel_id=1, source_target_pairs={{0,36},{1,37},{2,38},{3,39},{4,40},{5,41},{6,42},{7,43},{8,44},{9,... | collective-permute-start | bytes 786440 | tf_op jit(solution)/shard_map/ppermute | solution.py:175

commit v4 on v3

--- a/solution.py
+++ b/solution.py
@@ -44,12 +44,9 @@
     for pick in range(PICKS):
         slot = slots[turn, pick]
         rows = pl.ds(pick * TILE, TILE)
-        for side, held in enumerate((near_ref, far_ref)):
-
-            @pl.when(slot // PLANE == side)
-            def _():
-                k_sel[rows, :] = held[slot % PLANE, :, :HEAD_SIZE]
-                v_sel[rows, :HEAD_SIZE] = held[slot % PLANE, :, HEAD_SIZE:]
+        tile = jnp.where(slot < PLANE, near_ref[slot % PLANE], far_ref[slot % PLANE])
+        k_sel[rows, :] = tile[:, :HEAD_SIZE]
+        v_sel[rows, :HEAD_SIZE] = tile[:, HEAD_SIZE:]
 
     v_sel[:, HEAD_SIZE:] = jnp.ones((PICKS * TILE, HEAD_SIZE), jnp.bfloat16)
 
@@ -114,6 +111,34 @@
     )(heads, *pieces)
 
 
+def split_kernel(heads, queries_ref, *refs):
+    copies = []
+    for turn in range(SIDE):
+        columns = pl.ds(pl.multiple_of(heads[turn] * WIDE, WIDE), WIDE)
+        copies.append(
+            pltpu.make_async_copy(queries_ref.at[:, columns], refs[turn], refs[SIDE].at[turn])
+        )
+        copies[-1].start()
+    for copy in copies:
+        copy.wait()
+
+
+def split(heads, queries):
+    return list(
+        pl.pallas_call(
+            split_kernel,
+            out_shape=[jax.ShapeDtypeStruct((TILE, WIDE), jnp.bfloat16)] * SIDE,
+            in_specs=[SMEM, pl.BlockSpec(memory_space=pl.ANY)],
+            out_specs=[VMEM] * SIDE,
+            scratch_shapes=[pltpu.SemaphoreType.DMA((SIDE,))],
+            compiler_params=pltpu.CompilerParams(vmem_limit_bytes=6 * 1024 * 1024),
+            cost_estimate=pl.CostEstimate(
+                flops=0, bytes_accessed=2 * 1024 * 1024, transcendentals=0
+            ),
+        )(heads, queries)
+    )
+
+
 def repeat_kernel(held_ref, sent_ref, sems):
     copies = []
     for slot in range(PLANE):
@@ -140,7 +165,8 @@
 def on_device(queries, keys, values, block_pairs):
     queries, keys, values = queries[0], keys[0], values[0]
     place = lax.axis_index("dp")
-    half, row, column = place // PLANE, place // SIDE % SIDE, place % SIDE
+    half, row, column = place >> 4, (place >> 2) & 3, place & 3
+    turns = jnp.arange(SIDE, dtype=jnp.int32)
     groups = [[h * PLANE + i for i in range(PLANE)] for h in range(2)]
 
     def head_columns(array, head):
@@ -156,21 +182,21 @@
         ]
     )
     far = lax.ppermute(kv, AXES, route(0, 1, 0))
+    pairs = lax.ppermute(block_pairs[0, :, 1].reshape(TILES, PICKS), AXES, route(-1, 0, 0))
+    heads = (row + turns) & 3
+    kv, *pieces = lax.optimization_barrier((kv, *split(heads, queries)))
     near_landed = spread(repeated(kv, 0))
-    pairs = lax.ppermute(block_pairs[0, :, 1].reshape(TILES, PICKS), AXES, route(-1, 0, 0))
-    heads = (row + jnp.arange(SIDE, dtype=jnp.int32)) % SIDE
-    pieces = [lax.dynamic_slice_in_dim(queries, heads[turn] * WIDE, WIDE, 1) for turn in range(SIDE)]
     for turn in range(1, SIDE):
         pieces[turn] = lax.ppermute(pieces[turn], AXES, route(0, 0, turn))
     far_sent = repeated(far, 2 * 10**10)
-    far_sent, near_landed, pairs, *pieces = lax.optimization_barrier(
-        (far_sent, near_landed, pairs, *pieces)
+    far_sent, near_landed, pairs, pieces[1], pieces[3] = lax.optimization_barrier(
+        (far_sent, near_landed, pairs, pieces[1], pieces[3])
     )
     far_landed = spread(far_sent)
 
-    blocks = half * PLANE + (row - jnp.arange(SIDE, dtype=jnp.int32)) % SIDE * SIDE + column
+    blocks = half * PLANE + ((row - turns) & 3) * SIDE + column
     chosen = jnp.take(pairs, blocks, axis=0)
-    slots = (chosen % PLANE) + ((chosen // PLANE) ^ half) * PLANE
+    slots = (chosen & 15) + ((chosen >> 4) ^ half) * PLANE
     mixed = attention(slots, pieces, near_landed, far_landed)
     back = [lax.ppermute(mixed[turn], AXES, route(1, 0, -turn)) for turn in range(SIDE)]
     return assemble(heads, back)[None]

time: 110 us -> 108 us (0.982)
  waiting for transfers between devices: 31.4 us -> 36.6 us
  starting transfers between devices: 58.7 us -> 55.9 us
  between operations: 2.8 us -> 0.21 us
  local copies, waits for them, and re-layouts: 3.59 us -> 2.4 us
    ppermute x3, waiting for transfers between devices: 5.36 us -> 21.9 us  [on_device(): pieces[turn] = lax.ppermute(pieces[turn], AXES, route(0, 0, turn))]
    all_to_all x2, waiting for transfers between devices: 12.3 us -> 0.01 us  [spread(): return lax.all_to_all(sent, 'dp', 0, 0, axis_index_groups=groups)]
    ppermute x4, starting transfers between devices: 13 us -> 10.6 us  [on_device(): lax.ppermute(mixed[turn], AXES, route(1, 0, -turn))]
    dynamic_slice x1 -> x0, local copies, waits for them, and re-layouts: 1.27 us -> none  [on_device(): lax.dynamic_slice_in_dim(queries, heads[turn] * WIDE, WIDE, 1)]
  transfers between devices with their start and end apart: 11 -> 11, of which waited for: 8 -> 6; matrix products, arithmetic and copies ran while one was open for 3% -> 1% of each run, Pallas kernels for 2% -> 3%
where the time goes in v4:
time: 108 us; the launch traced here: 107 us
  starting transfers between devices  55.9 us (52%)
  waiting for transfers between devices  36.6 us (34%)
  Pallas kernels  11.7 us (11%)
  local copies, waits for them, and re-layouts  2.4 us (2%)
    ppermute x3, waiting for transfers between devices, on_device(): pieces[turn] = lax.ppermute(pieces[turn], AXES, route(0, 0, turn))  21.9 us
    ppermute x1, starting transfers between devices, on_device(): far = lax.ppermute(kv, AXES, route(0, 1, 0))  15.7 us
    ppermute x4, waiting for transfers between devices, on_device(): lax.ppermute(mixed[turn], AXES, route(1, 0, -turn))  14.7 us
    all_to_all x2, starting transfers between devices, spread(): return lax.all_to_all(sent, 'dp', 0, 0, axis_index_groups=groups)  13.3 us
    ppermute x3, starting transfers between devices, on_device(): pieces[turn] = lax.ppermute(pieces[turn], AXES, route(0, 0, turn))  11.9 us
    ppermute x4, starting transfers between devices, on_device(): lax.ppermute(mixed[turn], AXES, route(1, 0, -turn))  10.6 us
    pallas_call x1, Pallas kernels, attention(): pl.pallas_call(attention_kernel, out_shape=[jax.ShapeDtypeStruct((TILE, W...  7.28 us
    ppermute x1, starting transfers between devices, on_device(): lax.ppermute(block_pairs[0, :, 1].reshape(TILES, PICKS), AXES, route(-1,...  4.25 us
  transfers between devices with their start and end apart: 11, of which 6 were waited for; matrix products, arithmetic and copies ran while one was open for 1% of the time, Pallas kernels for 3%

profile of v4, /device:TPU:6, one launch (start us, length us, event | category | flops | bytes accessed | tf_op | source)
XLA Modules:
  0.0 107.0 jit_solution(15797142153635358196)
XLA Ops:
  0.0 0.0 copy-start
  0.0 0.9 fusion.2
  0.9 0.8 fusion.1
  1.8 15.7 %collective-permute-start = (bf16[4,128,256]{2,1,0:T(8,128)(2,1)S(1)}, bf16[4,128,256]{2,1,0:T(8,128)(2,1)S(1)}, u32[]{:S(2)}, u32[]{:S(2)}) collective-permute-start(bf16[4,128,256]{2,1,0:T(8,128)(2,1)S(1)} %pad_maximum_fusion.held_ref), channel_id=1, source_target_pairs={{0,16},{1,17},{2,18},{3,19},{4,20},{5,21},{6,22},{7,23},{8,24},{9,... | collective-permute-start | bytes 786440 | tf_op jit(solution)/shard_map/ppermute | solution.py:184
  17.6 0.0 copy-done
  17.6 0.7 shard_map.47
  18.3 1.1 %shard_map.48 = bf16[16,128,256]{2,1,0:T(8,128)(2,1)} custom-call(bf16[4,128,256]{2,1,0:T(8,128)(2,1)S(1)} %pad_maximum_fusion.held_ref), custom_call_target="tpu_custom_call" | custom-call | bytes 1310720 | tf_op jit(solution)/shard_map/pallas_call | solution.py:154
  19.4 0.0 copy-start.1
  19.4 7.4 %all-to-all-start = ((bf16[16,128,256]{2,1,0:T(8,128)(2,1)}), bf16[16,128,256]{2,1,0:T(8,128)(2,1)S(1)}, u32[]{:S(2)}, u32[]{:S(2)}) async-start(bf16[16,128,256]{2,1,0:T(8,128)(2,1)} %shard_map.48), calls=%async_computation | async-start | bytes 2097152 | tf_op jit(solution)/shard_map/all_to_all | solution.py:176
  26.8 0.0 copy-done.1
  26.9 0.1 reshape_squeeze.3
  26.9 4.3 %collective-permute-start.1 = (s32[32,8]{1,0:T(8,128)S(1)}, s32[32,8]{1,0:T(8,128)S(1)}, u32[]{:S(2)}, u32[]{:S(2)}) collective-permute-start(s32[32,8]{1,0:T(8,128)S(1)} %reshape_squeeze.3), channel_id=1, source_target_pairs={{0,480},{1,481},{2,482},{3,483},{4,484},{5,485},{6,486},{7,487},{8... | collective-permute-start | bytes 3080 | tf_op jit(solution)/shard_map/ppermute | solution.py:185
  31.2 3.4 %collective-permute-start.2 = (bf16[128,1024]{1,0:T(8,128)(2,1)S(1)}, bf16[128,1024]{1,0:T(8,128)(2,1)S(1)}, u32[]{:S(2)}, u32[]{:S(2)}) collective-permute-start(bf16[128,1024]{1,0:T(8,128)(2,1)S(1)} %get-tuple-element.28), channel_id=1, source_target_pairs={{0,4},{1,5},{2,6},{3,7},{4,8},{5,9},{6,10},{7,11},{8,12},{9,13},{1... | collective-permute-start | bytes 786440 | tf_op jit(solution)/shard_map/ppermute | solution.py:190
  34.6 3.7 %collective-permute-start.3 = (bf16[128,1024]{1,0:T(8,128)(2,1)S(1)}, bf16[128,1024]{1,0:T(8,128)(2,1)S(1)}, u32[]{:S(2)}, u32[]{:S(2)}) collective-permute-start(bf16[128,1024]{1,0:T(8,128)(2,1)S(1)} %get-tuple-element.29), channel_id=1, source_target_pairs={{0,12},{1,13},{2,14},{3,15},{4,0},{5,1},{6,2},{7,3},{8,4},{9,5},{1... | collective-permute-start | bytes 786440 | tf_op jit(solution)/shard_map/ppermute | solution.py:190
  38.3 0.0 collective-permute-done.held_ref
  38.3 1.1 %shard_map.46 = bf16[16,128,256]{2,1,0:T(8,128)(2,1)} custom-call(bf16[4,128,256]{2,1,0:T(8,128)(2,1)S(1)} %collective-permute-done.held_ref), custom_call_target="tpu_custom_call" | custom-call | flops 20000000000 | bytes 1310720 | tf_op jit(solution)/shard_map/pallas_call | solution.py:154
  39.4 0.0 collective-permute-done.1
  39.4 7.0 %collective-permute-done.2.refs_1_ = bf16[128,1024]{1,0:T(8,128)(2,1)S(1)} collective-permute-done((bf16[128,1024]{1,0:T(8,128)(2,1)S(1)}, bf16[128,1024]{1,0:T(8,128)(2,1)S(1)}, u32[]{:S(2)}, u32[]{:S(2)}) %collective-permute-start.2) | collective-permute-done | bytes 262176 | tf_op jit(solution)/shard_map/ppermute | solution.py:190
  46.4 0.0 collective-permute-done.3.refs_3_
  46.4 0.0 all-to-all-done.refs_4_
  46.4 5.9 %all-to-all-start.1 = ((bf16[16,128,256]{2,1,0:T(8,128)(2,1)}), bf16[16,128,256]{2,1,0:T(8,128)(2,1)S(1)}, u32[]{:S(2)}, u32[]{:S(2)}) async-start(bf16[16,128,256]{2,1,0:T(8,128)(2,1)} %shard_map.46), calls=%async_computation.1 | async-start | bytes 2097152 | tf_op jit(solution)/shard_map/all_to_all | solution.py:176
  52.3 4.9 %collective-permute-start.4 = (bf16[128,1024]{1,0:T(8,128)(2,1)S(1)}, bf16[128,1024]{1,0:T(8,128)(2,1)}, u32[]{:S(2)}, u32[]{:S(2)}) collective-permute-start(bf16[128,1024]{1,0:T(8,128)(2,1)S(1)} %get-tuple-element.33), channel_id=1, source_target_pairs={{0,8},{1,9},{2,10},{3,11},{4,12},{5,13},{6,14},{7,15},{8,0},{9,1},... | collective-permute-start | bytes 786440 | tf_op jit(solution)/shard_map/ppermute | solution.py:190
  57.3 0.6 gather_fusion
  57.8 0.1 multiply_add_fusion.slots
  57.9 14.9 %collective-permute-done.4.refs_2_ = bf16[128,1024]{1,0:T(8,128)(2,1)} collective-permute-done((bf16[128,1024]{1,0:T(8,128)(2,1)S(1)}, bf16[128,1024]{1,0:T(8,128)(2,1)}, u32[]{:S(2)}, u32[]{:S(2)}) %collective-permute-start.4) | collective-permute-done | bytes 262176 | tf_op jit(solution)/shard_map/ppermute | solution.py:190
  72.8 0.0 all-to-all-done.1.refs_5_
  72.8 7.3 %shard_map.49 = (bf16[128,1024]{1,0:T(8,128)(2,1)S(1)}, bf16[128,1024]{1,0:T(8,128)(2,1)S(1)}, bf16[128,1024]{1,0:T(8,128)(2,1)S(1)}, bf16[128,1024]{1,0:T(8,128)(2,1)S(1)}) custom-call(s32[4,8]{1,0:T(4,128)S(1)} %multiply_add_fusion.slots, bf16[128,1024]{1,0:T(8,128)(2,1)S(1)} %get-tuple-element.31.refs_0_, ...), custom_call_target="tpu_custom_call" | custom-call | flops 2147483648 | bytes 4194304 | tf_op jit(solution)/shard_map/pallas_call | solution.py:73
  80.0 1.9 %collective-permute-start.5 = (bf16[128,1024]{1,0:T(8,128)(2,1)S(1)}, bf16[128,1024]{1,0:T(8,128)(2,1)S(1)}, u32[]{:S(2)}, u32[]{:S(2)}) collective-permute-start(bf16[128,1024]{1,0:T(8,128)(2,1)S(1)} %get-tuple-element.37), channel_id=1, source_target_pairs={{0,32},{1,33},{2,34},{3,35},{4,36},{5,37},{6,38},{7,39},{8,40},{9,... | collective-permute-start | bytes 786440 | tf_op jit(solution)/shard_map/ppermute | solution.py:201
  82.0 3.9 %collective-permute-start.6 = (bf16[128,1024]{1,0:T(8,128)(2,1)S(1)}, bf16[128,1024]{1,0:T(8,128)(2,1)S(1)}, u32[]{:S(2)}, u32[]{:S(2)}) collective-permute-start(bf16[128,1024]{1,0:T(8,128)(2,1)S(1)} %get-tuple-element.38), channel_id=1, source_target_pairs={{0,44},{1,45},{2,46},{3,47},{4,32},{5,33},{6,34},{7,35},{8,36},{9,... | collective-permute-start | bytes 786440 | tf_op jit(solution)/shard_map/ppermute | solution.py:201
  85.9 2.7 %collective-permute-start.7 = (bf16[128,1024]{1,0:T(8,128)(2,1)S(1)}, bf16[128,1024]{1,0:T(8,128)(2,1)S(1)}, u32[]{:S(2)}, u32[]{:S(2)}) collective-permute-start(bf16[128,1024]{1,0:T(8,128)(2,1)S(1)} %get-tuple-element.39), channel_id=1, source_target_pairs={{0,40},{1,41},{2,42},{3,43},{4,44},{5,45},{6,46},{7,47},{8,32},{9,... | collective-permute-start | bytes 786440 | tf_op jit(solution)/shard_map/ppermute | solution.py:201
  88.6 2.1 %collective-permute-start.8 = (bf16[128,1024]{1,0:T(8,128)(2,1)S(1)}, bf16[128,1024]{1,0:T(8,128)(2,1)S(1)}, u32[]{:S(2)}, u32[]{:S(2)}) collective-permute-start(bf16[128,1024]{1,0:T(8,128)(2,1)S(1)} %get-tuple-element.40), channel_id=1, source_target_pairs={{0,36},{1,37},{2,38},{3,39},{4,40},{5,41},{6,42},{7,43},{8,44},{9,... | collective-permute-start | bytes 786440 | tf_op jit(solution)/shard_map/ppermute | solution.py:201
  90.7 3.6 %collective-permute-done.5.refs_0_ = bf16[128,1024]{1,0:T(8,128)(2,1)S(1)} collective-permute-done((bf16[128,1024]{1,0:T(8,128)(2,1)S(1)}, bf16[128,1024]{1,0:T(8,128)(2,1)S(1)}, u32[]{:S(2)}, u32[]{:S(2)}) %collective-permute-start.5) | collective-permute-done | bytes 262176 | tf_op jit(solution)/shard_map/ppermute | solution.py:201
  94.3 2.9 %collective-permute-done.6.refs_1_ = bf16[128,1024]{1,0:T(8,128)(2,1)S(1)} collective-permute-done((bf16[128,1024]{1,0:T(8,128)(2,1)S(1)}, bf16[128,1024]{1,0:T(8,128)(2,1)S(1)}, u32[]{:S(2)}, u32[]{:S(2)}) %collective-permute-start.6) | collective-permute-done | bytes 262176 | tf_op jit(solution)/shard_map/ppermute | solution.py:201
  97.2 5.5 %collective-permute-done.7.refs_2_ = bf16[128,1024]{1,0:T(8,128)(2,1)S(1)} collective-permute-done((bf16[128,1024]{1,0:T(8,128)(2,1)S(1)}, bf16[128,1024]{1,0:T(8,128)(2,1)S(1)}, u32[]{:S(2)}, u32[]{:S(2)}) %collective-permute-start.7) | collective-permute-done | bytes 262176 | tf_op jit(solution)/shard_map/ppermute | solution.py:201
  102.7 2.7 %collective-permute-done.8.refs_3_ = bf16[128,1024]{1,0:T(8,128)(2,1)S(1)} collective-permute-done((bf16[128,1024]{1,0:T(8,128)(2,1)S(1)}, bf16[128,1024]{1,0:T(8,128)(2,1)S(1)}, u32[]{:S(2)}, u32[]{:S(2)}) %collective-permute-start.8) | collective-permute-done | bytes 262176 | tf_op jit(solution)/shard_map/ppermute | solution.py:201
  105.4 1.5 %shard_map.50 = bf16[128,4096]{1,0:T(8,128)(2,1)} custom-call(s32[4]{0:T(128)S(1)} %add_and_fusion.heads, bf16[128,1024]{1,0:T(8,128)(2,1)S(1)} %collective-permute-done.5.refs_0_, bf16[128,1024]{1,0:T(8,128)(2,1)S(1)} %collective-permute-done.6.refs_1_, bf16[128,1024]{1,0:T(8,128)(2,1)S(1)} %collective-permute-done.7.refs_2_, ...), custom_call_target="tpu_custom_call" | custom-call | bytes 2097152 | tf_op jit(solution)/shard_map/pallas_call | solution.py:103
  (8 shorter events, 0.1 us)
Async XLA Ops:
  0.0 17.6 %copy-start = (bf16[1,128,4096]{2,1,0:T(8,128)(2,1)S(1)}, bf16[1,128,4096]{2,1,0:T(8,128)(2,1)}, u32[]{:S(2)}) copy-start(bf16[1,128,4096]{2,1,0:T(8,128)(2,1)} %param.4) | copy-start | bytes 3145732
  1.8 36.4 %collective-permute-start = (bf16[4,128,256]{2,1,0:T(8,128)(2,1)S(1)}, bf16[4,128,256]{2,1,0:T(8,128)(2,1)S(1)}, u32[]{:S(2)}, u32[]{:S(2)}) collective-permute-start(bf16[4,128,256]{2,1,0:T(8,128)(2,1)S(1)} %pad_maximum_fusion.held_ref), channel_id=1, source_target_pairs={{0,16},{1,17},{2,18},{3,19},{4,20},{5,21},{6,22},{7,23},{8,24},{9,... | collective-permute-start | bytes 786440 | tf_op jit(solution)/shard_map/ppermute | solution.py:184
  19.4 7.4 %copy-start.1 = (s32[1,256,2]{1,2,0:T(2,128)S(1)}, s32[1,256,2]{1,2,0:T(2,128)}, u32[]{:S(2)}) copy-start(s32[1,256,2]{1,2,0:T(2,128)} %param.7) | copy-start | bytes 6148
  19.4 27.0 %all-to-all-start = ((bf16[16,128,256]{2,1,0:T(8,128)(2,1)}), bf16[16,128,256]{2,1,0:T(8,128)(2,1)S(1)}, u32[]{:S(2)}, u32[]{:S(2)}) async-start(bf16[16,128,256]{2,1,0:T(8,128)(2,1)} %shard_map.48), calls=%async_computation | async-start | bytes 2097152 | tf_op jit(solution)/shard_map/all_to_all | solution.py:176
  26.9 12.5 %collective-permute-start.1 = (s32[32,8]{1,0:T(8,128)S(1)}, s32[32,8]{1,0:T(8,128)S(1)}, u32[]{:S(2)}, u32[]{:S(2)}) collective-permute-start(s32[32,8]{1,0:T(8,128)S(1)} %reshape_squeeze.3), channel_id=1, source_target_pairs={{0,480},{1,481},{2,482},{3,483},{4,484},{5,485},{6,486},{7,487},{8... | collective-permute-start | bytes 3080 | tf_op jit(solution)/shard_map/ppermute | solution.py:185
  31.2 15.2 %collective-permute-start.2 = (bf16[128,1024]{1,0:T(8,128)(2,1)S(1)}, bf16[128,1024]{1,0:T(8,128)(2,1)S(1)}, u32[]{:S(2)}, u32[]{:S(2)}) collective-permute-start(bf16[128,1024]{1,0:T(8,128)(2,1)S(1)} %get-tuple-element.28), channel_id=1, source_target_pairs={{0,4},{1,5},{2,6},{3,7},{4,8},{5,9},{6,10},{7,11},{8,12},{9,13},{1... | collective-permute-start | bytes 786440 | tf_op jit(solution)/shard_map/ppermute | solution.py:190
  34.6 11.8 %collective-permute-start.3 = (bf16[128,1024]{1,0:T(8,128)(2,1)S(1)}, bf16[128,1024]{1,0:T(8,128)(2,1)S(1)}, u32[]{:S(2)}, u32[]{:S(2)}) collective-permute-start(bf16[128,1024]{1,0:T(8,128)(2,1)S(1)} %get-tuple-element.29), channel_id=1, source_target_pairs={{0,12},{1,13},{2,14},{3,15},{4,0},{5,1},{6,2},{7,3},{8,4},{9,5},{1... | collective-permute-start | bytes 786440 | tf_op jit(solution)/shard_map/ppermute | solution.py:190
  46.4 26.4 %all-to-all-start.1 = ((bf16[16,128,256]{2,1,0:T(8,128)(2,1)}), bf16[16,128,256]{2,1,0:T(8,128)(2,1)S(1)}, u32[]{:S(2)}, u32[]{:S(2)}) async-start(bf16[16,128,256]{2,1,0:T(8,128)(2,1)} %shard_map.46), calls=%async_computation.1 | async-start | bytes 2097152 | tf_op jit(solution)/shard_map/all_to_all | solution.py:176
  52.3 20.4 %collective-permute-start.4 = (bf16[128,1024]{1,0:T(8,128)(2,1)S(1)}, bf16[128,1024]{1,0:T(8,128)(2,1)}, u32[]{:S(2)}, u32[]{:S(2)}) collective-permute-start(bf16[128,1024]{1,0:T(8,128)(2,1)S(1)} %get-tuple-element.33), channel_id=1, source_target_pairs={{0,8},{1,9},{2,10},{3,11},{4,12},{5,13},{6,14},{7,15},{8,0},{9,1},... | collective-permute-start | bytes 786440 | tf_op jit(solution)/shard_map/ppermute | solution.py:190
  80.0 14.3 %collective-permute-start.5 = (bf16[128,1024]{1,0:T(8,128)(2,1)S(1)}, bf16[128,1024]{1,0:T(8,128)(2,1)S(1)}, u32[]{:S(2)}, u32[]{:S(2)}) collective-permute-start(bf16[128,1024]{1,0:T(8,128)(2,1)S(1)} %get-tuple-element.37), channel_id=1, source_target_pairs={{0,32},{1,33},{2,34},{3,35},{4,36},{5,37},{6,38},{7,39},{8,40},{9,... | collective-permute-start | bytes 786440 | tf_op jit(solution)/shard_map/ppermute | solution.py:201
  82.0 15.2 %collective-permute-start.6 = (bf16[128,1024]{1,0:T(8,128)(2,1)S(1)}, bf16[128,1024]{1,0:T(8,128)(2,1)S(1)}, u32[]{:S(2)}, u32[]{:S(2)}) collective-permute-start(bf16[128,1024]{1,0:T(8,128)(2,1)S(1)} %get-tuple-element.38), channel_id=1, source_target_pairs={{0,44},{1,45},{2,46},{3,47},{4,32},{5,33},{6,34},{7,35},{8,36},{9,... | collective-permute-start | bytes 786440 | tf_op jit(solution)/shard_map/ppermute | solution.py:201
  85.9 16.8 %collective-permute-start.7 = (bf16[128,1024]{1,0:T(8,128)(2,1)S(1)}, bf16[128,1024]{1,0:T(8,128)(2,1)S(1)}, u32[]{:S(2)}, u32[]{:S(2)}) collective-permute-start(bf16[128,1024]{1,0:T(8,128)(2,1)S(1)} %get-tuple-element.39), channel_id=1, source_target_pairs={{0,40},{1,41},{2,42},{3,43},{4,44},{5,45},{6,46},{7,47},{8,32},{9,... | collective-permute-start | bytes 786440 | tf_op jit(solution)/shard_map/ppermute | solution.py:201
  88.6 16.8 %collective-permute-start.8 = (bf16[128,1024]{1,0:T(8,128)(2,1)S(1)}, bf16[128,1024]{1,0:T(8,128)(2,1)S(1)}, u32[]{:S(2)}, u32[]{:S(2)}) collective-permute-start(bf16[128,1024]{1,0:T(8,128)(2,1)S(1)} %get-tuple-element.40), channel_id=1, source_target_pairs={{0,36},{1,37},{2,38},{3,39},{4,40},{5,41},{6,42},{7,43},{8,44},{9,... | collective-permute-start | bytes 786440 | tf_op jit(solution)/shard_map/ppermute | solution.py:201

commit v5 on v4

--- a/solution.py
+++ b/solution.py
@@ -1,3 +1,4 @@
+import functools
 import math
 
 import jax
@@ -33,11 +34,12 @@
     return pairs
 
 
-def attention_kernel(slots, *refs):
-    query_refs, near_ref, far_ref = refs[:SIDE], refs[SIDE], refs[SIDE + 1]
-    out_refs, k_sel, v_sel = refs[SIDE + 2 : 2 * SIDE + 2], refs[-2], refs[-1]
-    for turn in range(SIDE):
-        attend(slots, turn, query_refs[turn], near_ref, far_ref, out_refs[turn], k_sel, v_sel)
+def attention_kernel(turns, slots, *refs):
+    count = len(turns)
+    query_refs, near_ref, far_ref = refs[:count], refs[count], refs[count + 1]
+    out_refs, k_sel, v_sel = refs[count + 2 : 2 * count + 2], refs[-2], refs[-1]
+    for query_ref, out_ref, turn in zip(query_refs, out_refs, turns):
+        attend(slots, turn, query_ref, near_ref, far_ref, out_ref, k_sel, v_sel)
 
 
 def attend(slots, turn, query_ref, near_ref, far_ref, out_ref, k_sel, v_sel):
@@ -69,21 +71,22 @@
         ).astype(jnp.bfloat16)
 
 
-def attention(slots, queries, near, far):
+def attention(turns, slots, queries, near, far):
+    count = len(turns)
     return pl.pallas_call(
-        attention_kernel,
-        out_shape=[jax.ShapeDtypeStruct((TILE, WIDE), jnp.bfloat16)] * SIDE,
-        in_specs=[SMEM] + [VMEM] * (SIDE + 2),
-        out_specs=[VMEM] * SIDE,
+        functools.partial(attention_kernel, turns),
+        out_shape=[jax.ShapeDtypeStruct((TILE, WIDE), jnp.bfloat16)] * count,
+        in_specs=[SMEM] + [VMEM] * (count + 2),
+        out_specs=[VMEM] * count,
         scratch_shapes=[
             pltpu.VMEM((PICKS * TILE, HEAD_SIZE), jnp.bfloat16),
             pltpu.VMEM((PICKS * TILE, 2 * HEAD_SIZE), jnp.bfloat16),
         ],
         compiler_params=pltpu.CompilerParams(vmem_limit_bytes=24 * 1024 * 1024),
         cost_estimate=pl.CostEstimate(
-            flops=2 * 2 * SIDE * GROUP * TILE * PICKS * TILE * HEAD_SIZE,
-            bytes_accessed=4 * 1024 * 1024,
-            transcendentals=SIDE * GROUP * TILE * PICKS * TILE,
+            flops=2 * 2 * count * GROUP * TILE * PICKS * TILE * HEAD_SIZE,
+            bytes_accessed=count * 1024 * 1024,
+            transcendentals=count * GROUP * TILE * PICKS * TILE,
         ),
     )(slots, *queries, near, far)
 
@@ -166,7 +169,7 @@
     queries, keys, values = queries[0], keys[0], values[0]
     place = lax.axis_index("dp")
     half, row, column = place >> 4, (place >> 2) & 3, place & 3
-    turns = jnp.arange(SIDE, dtype=jnp.int32)
+    steps = jnp.arange(SIDE, dtype=jnp.int32)
     groups = [[h * PLANE + i for i in range(PLANE)] for h in range(2)]
 
     def head_columns(array, head):
@@ -183,7 +186,7 @@
     )
     far = lax.ppermute(kv, AXES, route(0, 1, 0))
     pairs = lax.ppermute(block_pairs[0, :, 1].reshape(TILES, PICKS), AXES, route(-1, 0, 0))
-    heads = (row + turns) & 3
+    heads = (row + steps) & 3
     kv, *pieces = lax.optimization_barrier((kv, *split(heads, queries)))
     near_landed = spread(repeated(kv, 0))
     for turn in range(1, SIDE):
@@ -194,11 +197,15 @@
     )
     far_landed = spread(far_sent)
 
-    blocks = half * PLANE + ((row - turns) & 3) * SIDE + column
+    blocks = half * PLANE + ((row - steps) & 3) * SIDE + column
     chosen = jnp.take(pairs, blocks, axis=0)
     slots = (chosen & 15) + ((chosen >> 4) ^ half) * PLANE
-    mixed = attention(slots, pieces, near_landed, far_landed)
-    back = [lax.ppermute(mixed[turn], AXES, route(1, 0, -turn)) for turn in range(SIDE)]
+    back = [None] * SIDE
+    for turns in ((1, 3), (2, 0)):
+        mixed = attention(turns, slots, [pieces[turn] for turn in turns], near_landed, far_landed)
+        for turn, rows in zip(turns, mixed):
+            back[turn] = lax.ppermute(rows, AXES, route(1, 0, -turn))
+        slots, mixed = lax.optimization_barrier((slots, mixed))
     return assemble(heads, back)[None]
 
 

time: 108 us -> 106 us (0.981)
  the two profiles are of different devices: /device:TPU:6 before, /device:TPU:4 now
where the time goes in v5:
time: 106 us
  starting transfers between devices  61.1 us (58%)
  waiting for transfers between devices  29.4 us (28%)
  Pallas kernels  12.4 us (12%)
  local copies, waits for them, and re-layouts  2.4 us (2%)
    ppermute x4, starting transfers between devices, on_device(): back[turn] = lax.ppermute(rows, AXES, route(1, 0, -turn))  15.9 us
    ppermute x1, starting transfers between devices, on_device(): far = lax.ppermute(kv, AXES, route(0, 1, 0))  15.7 us
    all_to_all x2, starting transfers between devices, spread(): return lax.all_to_all(sent, 'dp', 0, 0, axis_index_groups=groups)  13.3 us
    ppermute x4, waiting for transfers between devices, on_device(): back[turn] = lax.ppermute(rows, AXES, route(1, 0, -turn))  13.1 us
    ppermute x3, starting transfers between devices, on_device(): pieces[turn] = lax.ppermute(pieces[turn], AXES, route(0, 0, turn))  11.9 us
    all_to_all x2, waiting for transfers between devices, spread(): return lax.all_to_all(sent, 'dp', 0, 0, axis_index_groups=groups)  9.26 us
    pallas_call x2, Pallas kernels, attention(): pl.pallas_call(functools.partial(attention_kernel, turns), out_shape=[jax...  7.95 us
    ppermute x3, waiting for transfers between devices, on_device(): pieces[turn] = lax.ppermute(pieces[turn], AXES, route(0, 0, turn))  7.02 us
  transfers between devices with their start and end apart: 11, of which 5 were waited for; matrix products, arithmetic and copies ran while one was open for 1% of the time, Pallas kernels for 10%

profile of v5, /device:TPU:4, one launch (start us, length us, event | category | flops | bytes accessed | tf_op | source)
XLA Modules:
  0.0 105.7 jit_solution(12700393915517146681)
XLA Ops:
  0.0 0.0 copy-start
  0.0 0.9 fusion.2
  0.9 0.8 fusion.1
  1.8 15.7 %collective-permute-start = (bf16[4,128,256]{2,1,0:T(8,128)(2,1)S(1)}, bf16[4,128,256]{2,1,0:T(8,128)(2,1)S(1)}, u32[]{:S(2)}, u32[]{:S(2)}) collective-permute-start(bf16[4,128,256]{2,1,0:T(8,128)(2,1)S(1)} %pad_maximum_fusion.held_ref), channel_id=1, source_target_pairs={{0,16},{1,17},{2,18},{3,19},{4,20},{5,21},{6,22},{7,23},{8,24},{9,... | collective-permute-start | bytes 786440 | tf_op jit(solution)/shard_map/ppermute | solution.py:187
  17.6 0.0 copy-done
  17.6 0.7 shard_map.47
  18.3 1.1 %shard_map.48 = bf16[16,128,256]{2,1,0:T(8,128)(2,1)} custom-call(bf16[4,128,256]{2,1,0:T(8,128)(2,1)S(1)} %pad_maximum_fusion.held_ref), custom_call_target="tpu_custom_call" | custom-call | bytes 1310720 | tf_op jit(solution)/shard_map/pallas_call | solution.py:157
  19.4 0.0 copy-start.1
  19.4 7.5 %all-to-all-start = ((bf16[16,128,256]{2,1,0:T(8,128)(2,1)}), bf16[16,128,256]{2,1,0:T(8,128)(2,1)S(1)}, u32[]{:S(2)}, u32[]{:S(2)}) async-start(bf16[16,128,256]{2,1,0:T(8,128)(2,1)} %shard_map.48), calls=%async_computation | async-start | bytes 2097152 | tf_op jit(solution)/shard_map/all_to_all | solution.py:179
  26.9 0.0 copy-done.1
  26.9 0.1 reshape_squeeze.3
  27.0 4.3 %collective-permute-start.1 = (s32[32,8]{1,0:T(8,128)S(1)}, s32[32,8]{1,0:T(8,128)S(1)}, u32[]{:S(2)}, u32[]{:S(2)}) collective-permute-start(s32[32,8]{1,0:T(8,128)S(1)} %reshape_squeeze.3), channel_id=1, source_target_pairs={{0,480},{1,481},{2,482},{3,483},{4,484},{5,485},{6,486},{7,487},{8... | collective-permute-start | bytes 3080 | tf_op jit(solution)/shard_map/ppermute | solution.py:188
  31.2 3.4 %collective-permute-start.2 = (bf16[128,1024]{1,0:T(8,128)(2,1)S(1)}, bf16[128,1024]{1,0:T(8,128)(2,1)S(1)}, u32[]{:S(2)}, u32[]{:S(2)}) collective-permute-start(bf16[128,1024]{1,0:T(8,128)(2,1)S(1)} %get-tuple-element.29), channel_id=1, source_target_pairs={{0,4},{1,5},{2,6},{3,7},{4,8},{5,9},{6,10},{7,11},{8,12},{9,13},{1... | collective-permute-start | bytes 786440 | tf_op jit(solution)/shard_map/ppermute | solution.py:193
  34.6 3.7 %collective-permute-start.3 = (bf16[128,1024]{1,0:T(8,128)(2,1)S(1)}, bf16[128,1024]{1,0:T(8,128)(2,1)S(1)}, u32[]{:S(2)}, u32[]{:S(2)}) collective-permute-start(bf16[128,1024]{1,0:T(8,128)(2,1)S(1)} %get-tuple-element.30), channel_id=1, source_target_pairs={{0,12},{1,13},{2,14},{3,15},{4,0},{5,1},{6,2},{7,3},{8,4},{9,5},{1... | collective-permute-start | bytes 786440 | tf_op jit(solution)/shard_map/ppermute | solution.py:193
  38.3 0.0 collective-permute-done.held_ref
  38.3 1.1 %shard_map.46 = bf16[16,128,256]{2,1,0:T(8,128)(2,1)} custom-call(bf16[4,128,256]{2,1,0:T(8,128)(2,1)S(1)} %collective-permute-done.held_ref), custom_call_target="tpu_custom_call" | custom-call | flops 20000000000 | bytes 1310720 | tf_op jit(solution)/shard_map/pallas_call | solution.py:157
  39.4 0.0 collective-permute-done.1
  39.4 7.0 %collective-permute-done.2.refs_0_ = bf16[128,1024]{1,0:T(8,128)(2,1)S(1)} collective-permute-done((bf16[128,1024]{1,0:T(8,128)(2,1)S(1)}, bf16[128,1024]{1,0:T(8,128)(2,1)S(1)}, u32[]{:S(2)}, u32[]{:S(2)}) %collective-permute-start.2) | collective-permute-done | bytes 262176 | tf_op jit(solution)/shard_map/ppermute | solution.py:193
  46.5 0.0 collective-permute-done.3.refs_1_
  46.5 0.0 all-to-all-done.refs_2_
  46.5 5.9 %all-to-all-start.1 = ((bf16[16,128,256]{2,1,0:T(8,128)(2,1)}), bf16[16,128,256]{2,1,0:T(8,128)(2,1)S(1)}, u32[]{:S(2)}, u32[]{:S(2)}) async-start(bf16[16,128,256]{2,1,0:T(8,128)(2,1)} %shard_map.46), calls=%async_computation.1 | async-start | bytes 2097152 | tf_op jit(solution)/shard_map/all_to_all | solution.py:179
  52.4 4.9 %collective-permute-start.4 = (bf16[128,1024]{1,0:T(8,128)(2,1)S(1)}, bf16[128,1024]{1,0:T(8,128)(2,1)}, u32[]{:S(2)}, u32[]{:S(2)}) collective-permute-start(bf16[128,1024]{1,0:T(8,128)(2,1)S(1)} %get-tuple-element.39), channel_id=1, source_target_pairs={{0,8},{1,9},{2,10},{3,11},{4,12},{5,13},{6,14},{7,15},{8,0},{9,1},... | collective-permute-start | bytes 786440 | tf_op jit(solution)/shard_map/ppermute | solution.py:193
  57.3 0.6 gather_fusion
  57.8 0.1 multiply_add_fusion.slots
  57.9 9.3 %all-to-all-done.1.refs_3_ = bf16[16,128,256]{2,1,0:T(8,128)(2,1)S(1)} async-done(((bf16[16,128,256]{2,1,0:T(8,128)(2,1)}), bf16[16,128,256]{2,1,0:T(8,128)(2,1)S(1)}, u32[]{:S(2)}, u32[]{:S(2)}) %all-to-all-start.1) | async-done | bytes 1048608 | tf_op jit(solution)/shard_map/all_to_all | solution.py:179
  67.2 3.8 %shard_map.49 = (bf16[128,1024]{1,0:T(8,128)(2,1)S(1)}, bf16[128,1024]{1,0:T(8,128)(2,1)S(1)}) custom-call(s32[4,8]{1,0:T(4,128)S(1)} %multiply_add_fusion.slots, bf16[128,1024]{1,0:T(8,128)(2,1)S(1)} %collective-permute-done.2.refs_0_, bf16[128,1024]{1,0:T(8,128)(2,1)S(1)} %collective-permute-done.3.refs_1_, ...), custom_call_target="tpu_custom_call" | custom-call | flops 1073741824 | bytes 2097152 | tf_op jit(solution)/shard_map/pallas_call | solution.py:76
  71.0 2.7 %collective-permute-start.6 = (bf16[128,1024]{1,0:T(8,128)(2,1)S(1)}, bf16[128,1024]{1,0:T(8,128)(2,1)S(1)}, u32[]{:S(2)}, u32[]{:S(2)}) collective-permute-start(bf16[128,1024]{1,0:T(8,128)(2,1)S(1)} %get-tuple-element.36), channel_id=1, source_target_pairs={{0,44},{1,45},{2,46},{3,47},{4,32},{5,33},{6,34},{7,35},{8,36},{9,... | collective-permute-start | bytes 786440 | tf_op jit(solution)/shard_map/ppermute | solution.py:207
  73.7 0.0 collective-permute-done.4.refs_0_
  73.7 4.2 %shard_map.50 = (bf16[128,1024]{1,0:T(8,128)(2,1)S(1)}, bf16[128,1024]{1,0:T(8,128)(2,1)S(1)}) custom-call(s32[4,8]{1,0:T(4,128)S(1)} %multiply_add_fusion.slots, bf16[128,1024]{1,0:T(8,128)(2,1)} %collective-permute-done.4.refs_0_, bf16[128,1024]{1,0:T(8,128)(2,1)S(1)} %get-tuple-element.40.refs_1_, bf16[16,128,256]{2,1,0:T(8,128)(2,1)S(1)} %all-to-all-done.refs_2_, ...), custom_call_target="tpu_custom_call" | custom-call | flops 1073741824 | bytes 2097152 | tf_op jit(solution)/shard_map/pallas_call | solution.py:76
  77.9 3.1 %collective-permute-start.5 = (bf16[128,1024]{1,0:T(8,128)(2,1)S(1)}, bf16[128,1024]{1,0:T(8,128)(2,1)S(1)}, u32[]{:S(2)}, u32[]{:S(2)}) collective-permute-start(bf16[128,1024]{1,0:T(8,128)(2,1)S(1)} %get-tuple-element.41), channel_id=1, source_target_pairs={{0,32},{1,33},{2,34},{3,35},{4,36},{5,37},{6,38},{7,39},{8,40},{9,... | collective-permute-start | bytes 786440 | tf_op jit(solution)/shard_map/ppermute | solution.py:207
  81.0 6.8 %collective-permute-start.7 = (bf16[128,1024]{1,0:T(8,128)(2,1)S(1)}, bf16[128,1024]{1,0:T(8,128)(2,1)S(1)}, u32[]{:S(2)}, u32[]{:S(2)}) collective-permute-start(bf16[128,1024]{1,0:T(8,128)(2,1)S(1)} %get-tuple-element.42), channel_id=1, source_target_pairs={{0,40},{1,41},{2,42},{3,43},{4,44},{5,45},{6,46},{7,47},{8,32},{9,... | collective-permute-start | bytes 786440 | tf_op jit(solution)/shard_map/ppermute | solution.py:207
  87.8 3.3 %collective-permute-start.8 = (bf16[128,1024]{1,0:T(8,128)(2,1)S(1)}, bf16[128,1024]{1,0:T(8,128)(2,1)S(1)}, u32[]{:S(2)}, u32[]{:S(2)}) collective-permute-start(bf16[128,1024]{1,0:T(8,128)(2,1)S(1)} %get-tuple-element.37), channel_id=1, source_target_pairs={{0,36},{1,37},{2,38},{3,39},{4,40},{5,41},{6,42},{7,43},{8,44},{9,... | collective-permute-start | bytes 786440 | tf_op jit(solution)/shard_map/ppermute | solution.py:207
  91.1 1.1 %collective-permute-done.5.refs_0_ = bf16[128,1024]{1,0:T(8,128)(2,1)S(1)} collective-permute-done((bf16[128,1024]{1,0:T(8,128)(2,1)S(1)}, bf16[128,1024]{1,0:T(8,128)(2,1)S(1)}, u32[]{:S(2)}, u32[]{:S(2)}) %collective-permute-start.5) | collective-permute-done | bytes 262176 | tf_op jit(solution)/shard_map/ppermute | solution.py:207
  92.2 0.0 collective-permute-done.6.refs_1_
  92.2 7.5 %collective-permute-done.7.refs_2_ = bf16[128,1024]{1,0:T(8,128)(2,1)S(1)} collective-permute-done((bf16[128,1024]{1,0:T(8,128)(2,1)S(1)}, bf16[128,1024]{1,0:T(8,128)(2,1)S(1)}, u32[]{:S(2)}, u32[]{:S(2)}) %collective-permute-start.7) | collective-permute-done | bytes 262176 | tf_op jit(solution)/shard_map/ppermute | solution.py:207
  99.7 4.5 %collective-permute-done.8.refs_3_ = bf16[128,1024]{1,0:T(8,128)(2,1)S(1)} collective-permute-done((bf16[128,1024]{1,0:T(8,128)(2,1)S(1)}, bf16[128,1024]{1,0:T(8,128)(2,1)S(1)}, u32[]{:S(2)}, u32[]{:S(2)}) %collective-permute-start.8) | collective-permute-done | bytes 262176 | tf_op jit(solution)/shard_map/ppermute | solution.py:207
  104.2 1.5 %shard_map.51 = bf16[128,4096]{1,0:T(8,128)(2,1)} custom-call(s32[4]{0:T(128)S(1)} %add_and_fusion.heads, bf16[128,1024]{1,0:T(8,128)(2,1)S(1)} %collective-permute-done.5.refs_0_, bf16[128,1024]{1,0:T(8,128)(2,1)S(1)} %collective-permute-done.6.refs_1_, bf16[128,1024]{1,0:T(8,128)(2,1)S(1)} %collective-permute-done.7.refs_2_, ...), custom_call_target="tpu_custom_call" | custom-call | bytes 2097152 | tf_op jit(solution)/shard_map/pallas_call | solution.py:106
  (8 shorter events, 0.1 us)
Async XLA Ops:
  0.0 17.6 %copy-start = (bf16[1,128,4096]{2,1,0:T(8,128)(2,1)S(1)}, bf16[1,128,4096]{2,1,0:T(8,128)(2,1)}, u32[]{:S(2)}) copy-start(bf16[1,128,4096]{2,1,0:T(8,128)(2,1)} %param.4) | copy-start | bytes 3145732
  1.8 36.5 %collective-permute-start = (bf16[4,128,256]{2,1,0:T(8,128)(2,1)S(1)}, bf16[4,128,256]{2,1,0:T(8,128)(2,1)S(1)}, u32[]{:S(2)}, u32[]{:S(2)}) collective-permute-start(bf16[4,128,256]{2,1,0:T(8,128)(2,1)S(1)} %pad_maximum_fusion.held_ref), channel_id=1, source_target_pairs={{0,16},{1,17},{2,18},{3,19},{4,20},{5,21},{6,22},{7,23},{8,24},{9,... | collective-permute-start | bytes 786440 | tf_op jit(solution)/shard_map/ppermute | solution.py:187
  19.4 7.5 %copy-start.1 = (s32[1,256,2]{1,2,0:T(2,128)S(1)}, s32[1,256,2]{1,2,0:T(2,128)}, u32[]{:S(2)}) copy-start(s32[1,256,2]{1,2,0:T(2,128)} %param.7) | copy-start | bytes 6148
  19.4 27.1 %all-to-all-start = ((bf16[16,128,256]{2,1,0:T(8,128)(2,1)}), bf16[16,128,256]{2,1,0:T(8,128)(2,1)S(1)}, u32[]{:S(2)}, u32[]{:S(2)}) async-start(bf16[16,128,256]{2,1,0:T(8,128)(2,1)} %shard_map.48), calls=%async_computation | async-start | bytes 2097152 | tf_op jit(solution)/shard_map/all_to_all | solution.py:179
  27.0 12.5 %collective-permute-start.1 = (s32[32,8]{1,0:T(8,128)S(1)}, s32[32,8]{1,0:T(8,128)S(1)}, u32[]{:S(2)}, u32[]{:S(2)}) collective-permute-start(s32[32,8]{1,0:T(8,128)S(1)} %reshape_squeeze.3), channel_id=1, source_target_pairs={{0,480},{1,481},{2,482},{3,483},{4,484},{5,485},{6,486},{7,487},{8... | collective-permute-start | bytes 3080 | tf_op jit(solution)/shard_map/ppermute | solution.py:188
  31.2 15.2 %collective-permute-start.2 = (bf16[128,1024]{1,0:T(8,128)(2,1)S(1)}, bf16[128,1024]{1,0:T(8,128)(2,1)S(1)}, u32[]{:S(2)}, u32[]{:S(2)}) collective-permute-start(bf16[128,1024]{1,0:T(8,128)(2,1)S(1)} %get-tuple-element.29), channel_id=1, source_target_pairs={{0,4},{1,5},{2,6},{3,7},{4,8},{5,9},{6,10},{7,11},{8,12},{9,13},{1... | collective-permute-start | bytes 786440 | tf_op jit(solution)/shard_map/ppermute | solution.py:193
  34.6 11.9 %collective-permute-start.3 = (bf16[128,1024]{1,0:T(8,128)(2,1)S(1)}, bf16[128,1024]{1,0:T(8,128)(2,1)S(1)}, u32[]{:S(2)}, u32[]{:S(2)}) collective-permute-start(bf16[128,1024]{1,0:T(8,128)(2,1)S(1)} %get-tuple-element.30), channel_id=1, source_target_pairs={{0,12},{1,13},{2,14},{3,15},{4,0},{5,1},{6,2},{7,3},{8,4},{9,5},{1... | collective-permute-start | bytes 786440 | tf_op jit(solution)/shard_map/ppermute | solution.py:193
  46.5 20.7 %all-to-all-start.1 = ((bf16[16,128,256]{2,1,0:T(8,128)(2,1)}), bf16[16,128,256]{2,1,0:T(8,128)(2,1)S(1)}, u32[]{:S(2)}, u32[]{:S(2)}) async-start(bf16[16,128,256]{2,1,0:T(8,128)(2,1)} %shard_map.46), calls=%async_computation.1 | async-start | bytes 2097152 | tf_op jit(solution)/shard_map/all_to_all | solution.py:179
  52.4 21.3 %collective-permute-start.4 = (bf16[128,1024]{1,0:T(8,128)(2,1)S(1)}, bf16[128,1024]{1,0:T(8,128)(2,1)}, u32[]{:S(2)}, u32[]{:S(2)}) collective-permute-start(bf16[128,1024]{1,0:T(8,128)(2,1)S(1)} %get-tuple-element.39), channel_id=1, source_target_pairs={{0,8},{1,9},{2,10},{3,11},{4,12},{5,13},{6,14},{7,15},{8,0},{9,1},... | collective-permute-start | bytes 786440 | tf_op jit(solution)/shard_map/ppermute | solution.py:193
  71.0 21.2 %collective-permute-start.6 = (bf16[128,1024]{1,0:T(8,128)(2,1)S(1)}, bf16[128,1024]{1,0:T(8,128)(2,1)S(1)}, u32[]{:S(2)}, u32[]{:S(2)}) collective-permute-start(bf16[128,1024]{1,0:T(8,128)(2,1)S(1)} %get-tuple-element.36), channel_id=1, source_target_pairs={{0,44},{1,45},{2,46},{3,47},{4,32},{5,33},{6,34},{7,35},{8,36},{9,... | collective-permute-start | bytes 786440 | tf_op jit(solution)/shard_map/ppermute | solution.py:207
  77.9 14.3 %collective-permute-start.5 = (bf16[128,1024]{1,0:T(8,128)(2,1)S(1)}, bf16[128,1024]{1,0:T(8,128)(2,1)S(1)}, u32[]{:S(2)}, u32[]{:S(2)}) collective-permute-start(bf16[128,1024]{1,0:T(8,128)(2,1)S(1)} %get-tuple-element.41), channel_id=1, source_target_pairs={{0,32},{1,33},{2,34},{3,35},{4,36},{5,37},{6,38},{7,39},{8,40},{9,... | collective-permute-start | bytes 786440 | tf_op jit(solution)/shard_map/ppermute | solution.py:207
  81.0 18.7 %collective-permute-start.7 = (bf16[128,1024]{1,0:T(8,128)(2,1)S(1)}, bf16[128,1024]{1,0:T(8,128)(2,1)S(1)}, u32[]{:S(2)}, u32[]{:S(2)}) collective-permute-start(bf16[128,1024]{1,0:T(8,128)(2,1)S(1)} %get-tuple-element.42), channel_id=1, source_target_pairs={{0,40},{1,41},{2,42},{3,43},{4,44},{5,45},{6,46},{7,47},{8,32},{9,... | collective-permute-start | bytes 786440 | tf_op jit(solution)/shard_map/ppermute | solution.py:207
  87.8 16.4 %collective-permute-start.8 = (bf16[128,1024]{1,0:T(8,128)(2,1)S(1)}, bf16[128,1024]{1,0:T(8,128)(2,1)S(1)}, u32[]{:S(2)}, u32[]{:S(2)}) collective-permute-start(bf16[128,1024]{1,0:T(8,128)(2,1)S(1)} %get-tuple-element.37), channel_id=1, source_target_pairs={{0,36},{1,37},{2,38},{3,39},{4,40},{5,41},{6,42},{7,43},{8,44},{9,... | collective-permute-start | bytes 786440 | tf_op jit(solution)/shard_map/ppermute | solution.py:207

commit v6 on v5

--- a/solution.py
+++ b/solution.py
@@ -192,8 +192,8 @@
     for turn in range(1, SIDE):
         pieces[turn] = lax.ppermute(pieces[turn], AXES, route(0, 0, turn))
     far_sent = repeated(far, 2 * 10**10)
-    far_sent, near_landed, pairs, pieces[1], pieces[3] = lax.optimization_barrier(
-        (far_sent, near_landed, pairs, pieces[1], pieces[3])
+    far_sent, near_landed, pieces[1], pieces[3] = lax.optimization_barrier(
+        (far_sent, near_landed, pieces[1], pieces[3])
     )
     far_landed = spread(far_sent)
 

time: 106 us -> 106 us (level)
  the two profiles are of different devices: /device:TPU:4 before, /device:TPU:6 now
where the time goes in v6:
time: 106 us; the launch traced here: 104 us
  starting transfers between devices  57.2 us (54%)
  waiting for transfers between devices  32.1 us (30%)
  Pallas kernels  12.4 us (12%)
  local copies, waits for them, and re-layouts  2.4 us (2%)
    ppermute x1, starting transfers between devices, on_device(): far = lax.ppermute(kv, AXES, route(0, 1, 0))  15.7 us
    ppermute x4, waiting for transfers between devices, on_device(): back[turn] = lax.ppermute(rows, AXES, route(1, 0, -turn))  14.5 us
    all_to_all x2, starting transfers between devices, spread(): return lax.all_to_all(sent, 'dp', 0, 0, axis_index_groups=groups)  13.2 us
    ppermute x3, waiting for transfers between devices, on_device(): pieces[turn] = lax.ppermute(pieces[turn], AXES, route(0, 0, turn))  12.5 us
    ppermute x3, starting transfers between devices, on_device(): pieces[turn] = lax.ppermute(pieces[turn], AXES, route(0, 0, turn))  11.9 us
    ppermute x4, starting transfers between devices, on_device(): back[turn] = lax.ppermute(rows, AXES, route(1, 0, -turn))  11.6 us
    pallas_call x2, Pallas kernels, attention(): pl.pallas_call(functools.partial(attention_kernel, turns), out_shape=[jax...  7.95 us
    all_to_all x2, waiting for transfers between devices, spread(): return lax.all_to_all(sent, 'dp', 0, 0, axis_index_groups=groups)  5.13 us
  transfers between devices with their start and end apart: 11, of which 7 were waited for; matrix products, arithmetic and copies ran while one was open for 1% of the time, Pallas kernels for 6%

profile of v6, /device:TPU:6, one launch (start us, length us, event | category | flops | bytes accessed | tf_op | source)
XLA Modules:
  0.0 104.4 jit_solution(12936235685629836298)
XLA Ops:
  0.0 0.0 copy-start
  0.0 0.9 fusion.1
  0.9 0.8 fusion.2
  1.8 15.7 %collective-permute-start.1 = (bf16[4,128,256]{2,1,0:T(8,128)(2,1)S(1)}, bf16[4,128,256]{2,1,0:T(8,128)(2,1)S(1)}, u32[]{:S(2)}, u32[]{:S(2)}) collective-permute-start(bf16[4,128,256]{2,1,0:T(8,128)(2,1)S(1)} %pad_maximum_fusion.held_ref), channel_id=1, source_target_pairs={{0,16},{1,17},{2,18},{3,19},{4,20},{5,21},{6,22},{7,23},{8,24},{9,... | collective-permute-start | bytes 786440 | tf_op jit(solution)/shard_map/ppermute | solution.py:187
  17.6 0.0 copy-done
  17.6 0.7 shard_map.47
  18.3 1.1 %shard_map.48 = bf16[16,128,256]{2,1,0:T(8,128)(2,1)} custom-call(bf16[4,128,256]{2,1,0:T(8,128)(2,1)S(1)} %pad_maximum_fusion.held_ref), custom_call_target="tpu_custom_call" | custom-call | bytes 1310720 | tf_op jit(solution)/shard_map/pallas_call | solution.py:157
  19.4 7.4 %all-to-all-start = ((bf16[16,128,256]{2,1,0:T(8,128)(2,1)}), bf16[16,128,256]{2,1,0:T(8,128)(2,1)S(1)}, u32[]{:S(2)}, u32[]{:S(2)}) async-start(bf16[16,128,256]{2,1,0:T(8,128)(2,1)} %shard_map.48), calls=%async_computation | async-start | bytes 2097152 | tf_op jit(solution)/shard_map/all_to_all | solution.py:179
  26.8 3.4 %collective-permute-start.2 = (bf16[128,1024]{1,0:T(8,128)(2,1)S(1)}, bf16[128,1024]{1,0:T(8,128)(2,1)S(1)}, u32[]{:S(2)}, u32[]{:S(2)}) collective-permute-start(bf16[128,1024]{1,0:T(8,128)(2,1)S(1)} %get-tuple-element.28), channel_id=1, source_target_pairs={{0,4},{1,5},{2,6},{3,7},{4,8},{5,9},{6,10},{7,11},{8,12},{9,13},{1... | collective-permute-start | bytes 786440 | tf_op jit(solution)/shard_map/ppermute | solution.py:193
  30.2 3.7 %collective-permute-start.3 = (bf16[128,1024]{1,0:T(8,128)(2,1)S(1)}, bf16[128,1024]{1,0:T(8,128)(2,1)S(1)}, u32[]{:S(2)}, u32[]{:S(2)}) collective-permute-start(bf16[128,1024]{1,0:T(8,128)(2,1)S(1)} %get-tuple-element.29), channel_id=1, source_target_pairs={{0,12},{1,13},{2,14},{3,15},{4,0},{5,1},{6,2},{7,3},{8,4},{9,5},{1... | collective-permute-start | bytes 786440 | tf_op jit(solution)/shard_map/ppermute | solution.py:193
  33.9 0.0 collective-permute-done.1.held_ref
  33.9 1.1 %shard_map.46 = bf16[16,128,256]{2,1,0:T(8,128)(2,1)} custom-call(bf16[4,128,256]{2,1,0:T(8,128)(2,1)S(1)} %collective-permute-done.1.held_ref), custom_call_target="tpu_custom_call" | custom-call | flops 20000000000 | bytes 1310720 | tf_op jit(solution)/shard_map/pallas_call | solution.py:157
  35.0 0.0 copy-start.1
  35.0 11.4 %collective-permute-done.2.refs_0_ = bf16[128,1024]{1,0:T(8,128)(2,1)S(1)} collective-permute-done((bf16[128,1024]{1,0:T(8,128)(2,1)S(1)}, bf16[128,1024]{1,0:T(8,128)(2,1)S(1)}, u32[]{:S(2)}, u32[]{:S(2)}) %collective-permute-start.2) | collective-permute-done | bytes 262176 | tf_op jit(solution)/shard_map/ppermute | solution.py:193
  46.4 0.0 collective-permute-done.3.refs_1_
  46.4 0.0 all-to-all-done.refs_2_
  46.4 5.8 %all-to-all-start.1 = ((bf16[16,128,256]{2,1,0:T(8,128)(2,1)}), bf16[16,128,256]{2,1,0:T(8,128)(2,1)S(1)}, u32[]{:S(2)}, u32[]{:S(2)}) async-start(bf16[16,128,256]{2,1,0:T(8,128)(2,1)} %shard_map.46), calls=%async_computation.1 | async-start | bytes 2097152 | tf_op jit(solution)/shard_map/all_to_all | solution.py:179
  52.2 0.0 copy-done.1
  52.2 0.1 reshape_squeeze.3
  52.3 4.7 %collective-permute-start = (s32[32,8]{1,0:T(8,128)S(1)}, s32[32,8]{1,0:T(8,128)S(1)}, u32[]{:S(2)}, u32[]{:S(2)}) collective-permute-start(s32[32,8]{1,0:T(8,128)S(1)} %reshape_squeeze.3), channel_id=1, source_target_pairs={{0,480},{1,481},{2,482},{3,483},{4,484},{5,485},{6,486},{7,487},{8... | collective-permute-start | bytes 3080 | tf_op jit(solution)/shard_map/ppermute | solution.py:188
  56.9 4.9 %collective-permute-start.4 = (bf16[128,1024]{1,0:T(8,128)(2,1)S(1)}, bf16[128,1024]{1,0:T(8,128)(2,1)}, u32[]{:S(2)}, u32[]{:S(2)}) collective-permute-start(bf16[128,1024]{1,0:T(8,128)(2,1)S(1)} %get-tuple-element.37), channel_id=1, source_target_pairs={{0,8},{1,9},{2,10},{3,11},{4,12},{5,13},{6,14},{7,15},{8,0},{9,1},... | collective-permute-start | bytes 786440 | tf_op jit(solution)/shard_map/ppermute | solution.py:193
  61.9 0.0 collective-permute-done
  61.9 0.6 gather_fusion
  62.5 0.1 multiply_add_fusion.slots
  62.5 5.1 %all-to-all-done.1.refs_3_ = bf16[16,128,256]{2,1,0:T(8,128)(2,1)S(1)} async-done(((bf16[16,128,256]{2,1,0:T(8,128)(2,1)}), bf16[16,128,256]{2,1,0:T(8,128)(2,1)S(1)}, u32[]{:S(2)}, u32[]{:S(2)}) %all-to-all-start.1) | async-done | bytes 1048608 | tf_op jit(solution)/shard_map/all_to_all | solution.py:179
  67.7 3.8 %shard_map.49 = (bf16[128,1024]{1,0:T(8,128)(2,1)S(1)}, bf16[128,1024]{1,0:T(8,128)(2,1)S(1)}) custom-call(s32[4,8]{1,0:T(4,128)S(1)} %multiply_add_fusion.slots, bf16[128,1024]{1,0:T(8,128)(2,1)S(1)} %collective-permute-done.2.refs_0_, bf16[128,1024]{1,0:T(8,128)(2,1)S(1)} %collective-permute-done.3.refs_1_, ...), custom_call_target="tpu_custom_call" | custom-call | flops 1073741824 | bytes 2097152 | tf_op jit(solution)/shard_map/pallas_call | solution.py:76
  71.5 1.1 %collective-permute-done.4.refs_0_ = bf16[128,1024]{1,0:T(8,128)(2,1)} collective-permute-done((bf16[128,1024]{1,0:T(8,128)(2,1)S(1)}, bf16[128,1024]{1,0:T(8,128)(2,1)}, u32[]{:S(2)}, u32[]{:S(2)}) %collective-permute-start.4) | collective-permute-done | bytes 262176 | tf_op jit(solution)/shard_map/ppermute | solution.py:193
  72.5 4.2 %shard_map.50 = (bf16[128,1024]{1,0:T(8,128)(2,1)S(1)}, bf16[128,1024]{1,0:T(8,128)(2,1)S(1)}) custom-call(s32[4,8]{1,0:T(4,128)S(1)} %multiply_add_fusion.slots, bf16[128,1024]{1,0:T(8,128)(2,1)} %collective-permute-done.4.refs_0_, bf16[128,1024]{1,0:T(8,128)(2,1)S(1)} %get-tuple-element.38.refs_1_, bf16[16,128,256]{2,1,0:T(8,128)(2,1)S(1)} %all-to-all-done.refs_2_, ...), custom_call_target="tpu_custom_call" | custom-call | flops 1073741824 | bytes 2097152 | tf_op jit(solution)/shard_map/pallas_call | solution.py:76
  76.7 1.9 %collective-permute-start.5 = (bf16[128,1024]{1,0:T(8,128)(2,1)S(1)}, bf16[128,1024]{1,0:T(8,128)(2,1)S(1)}, u32[]{:S(2)}, u32[]{:S(2)}) collective-permute-start(bf16[128,1024]{1,0:T(8,128)(2,1)S(1)} %get-tuple-element.39), channel_id=1, source_target_pairs={{0,32},{1,33},{2,34},{3,35},{4,36},{5,37},{6,38},{7,39},{8,40},{9,... | collective-permute-start | bytes 786440 | tf_op jit(solution)/shard_map/ppermute | solution.py:207
  78.6 3.3 %collective-permute-start.7 = (bf16[128,1024]{1,0:T(8,128)(2,1)S(1)}, bf16[128,1024]{1,0:T(8,128)(2,1)S(1)}, u32[]{:S(2)}, u32[]{:S(2)}) collective-permute-start(bf16[128,1024]{1,0:T(8,128)(2,1)S(1)} %get-tuple-element.40), channel_id=1, source_target_pairs={{0,40},{1,41},{2,42},{3,43},{4,44},{5,45},{6,46},{7,47},{8,32},{9,... | collective-permute-start | bytes 786440 | tf_op jit(solution)/shard_map/ppermute | solution.py:207
  81.9 4.6 %collective-permute-start.6 = (bf16[128,1024]{1,0:T(8,128)(2,1)S(1)}, bf16[128,1024]{1,0:T(8,128)(2,1)S(1)}, u32[]{:S(2)}, u32[]{:S(2)}) collective-permute-start(bf16[128,1024]{1,0:T(8,128)(2,1)S(1)} %get-tuple-element.34), channel_id=1, source_target_pairs={{0,44},{1,45},{2,46},{3,47},{4,32},{5,33},{6,34},{7,35},{8,36},{9,... | collective-permute-start | bytes 786440 | tf_op jit(solution)/shard_map/ppermute | solution.py:207
  86.5 1.9 %collective-permute-start.8 = (bf16[128,1024]{1,0:T(8,128)(2,1)S(1)}, bf16[128,1024]{1,0:T(8,128)(2,1)S(1)}, u32[]{:S(2)}, u32[]{:S(2)}) collective-permute-start(bf16[128,1024]{1,0:T(8,128)(2,1)S(1)} %get-tuple-element.35), channel_id=1, source_target_pairs={{0,36},{1,37},{2,38},{3,39},{4,40},{5,41},{6,42},{7,43},{8,44},{9,... | collective-permute-start | bytes 786440 | tf_op jit(solution)/shard_map/ppermute | solution.py:207
  88.4 2.6 %collective-permute-done.5.refs_0_ = bf16[128,1024]{1,0:T(8,128)(2,1)S(1)} collective-permute-done((bf16[128,1024]{1,0:T(8,128)(2,1)S(1)}, bf16[128,1024]{1,0:T(8,128)(2,1)S(1)}, u32[]{:S(2)}, u32[]{:S(2)}) %collective-permute-start.5) | collective-permute-done | bytes 262176 | tf_op jit(solution)/shard_map/ppermute | solution.py:207
  91.0 4.5 %collective-permute-done.7.refs_2_ = bf16[128,1024]{1,0:T(8,128)(2,1)S(1)} collective-permute-done((bf16[128,1024]{1,0:T(8,128)(2,1)S(1)}, bf16[128,1024]{1,0:T(8,128)(2,1)S(1)}, u32[]{:S(2)}, u32[]{:S(2)}) %collective-permute-start.7) | collective-permute-done | bytes 262176 | tf_op jit(solution)/shard_map/ppermute | solution.py:207
  95.6 1.7 %collective-permute-done.6.refs_1_ = bf16[128,1024]{1,0:T(8,128)(2,1)S(1)} collective-permute-done((bf16[128,1024]{1,0:T(8,128)(2,1)S(1)}, bf16[128,1024]{1,0:T(8,128)(2,1)S(1)}, u32[]{:S(2)}, u32[]{:S(2)}) %collective-permute-start.6) | collective-permute-done | bytes 262176 | tf_op jit(solution)/shard_map/ppermute | solution.py:207
  97.3 5.6 %collective-permute-done.8.refs_3_ = bf16[128,1024]{1,0:T(8,128)(2,1)S(1)} collective-permute-done((bf16[128,1024]{1,0:T(8,128)(2,1)S(1)}, bf16[128,1024]{1,0:T(8,128)(2,1)S(1)}, u32[]{:S(2)}, u32[]{:S(2)}) %collective-permute-start.8) | collective-permute-done | bytes 262176 | tf_op jit(solution)/shard_map/ppermute | solution.py:207
  102.9 1.5 %shard_map.51 = bf16[128,4096]{1,0:T(8,128)(2,1)} custom-call(s32[4]{0:T(128)S(1)} %add_and_fusion.heads, bf16[128,1024]{1,0:T(8,128)(2,1)S(1)} %collective-permute-done.5.refs_0_, bf16[128,1024]{1,0:T(8,128)(2,1)S(1)} %collective-permute-done.6.refs_1_, bf16[128,1024]{1,0:T(8,128)(2,1)S(1)} %collective-permute-done.7.refs_2_, ...), custom_call_target="tpu_custom_call" | custom-call | bytes 2097152 | tf_op jit(solution)/shard_map/pallas_call | solution.py:106
  (8 shorter events, 0.1 us)
Async XLA Ops:
  0.0 17.6 %copy-start = (bf16[1,128,4096]{2,1,0:T(8,128)(2,1)S(1)}, bf16[1,128,4096]{2,1,0:T(8,128)(2,1)}, u32[]{:S(2)}) copy-start(bf16[1,128,4096]{2,1,0:T(8,128)(2,1)} %param.4) | copy-start | bytes 3145732
  1.8 32.0 %collective-permute-start.1 = (bf16[4,128,256]{2,1,0:T(8,128)(2,1)S(1)}, bf16[4,128,256]{2,1,0:T(8,128)(2,1)S(1)}, u32[]{:S(2)}, u32[]{:S(2)}) collective-permute-start(bf16[4,128,256]{2,1,0:T(8,128)(2,1)S(1)} %pad_maximum_fusion.held_ref), channel_id=1, source_target_pairs={{0,16},{1,17},{2,18},{3,19},{4,20},{5,21},{6,22},{7,23},{8,24},{9,... | collective-permute-start | bytes 786440 | tf_op jit(solution)/shard_map/ppermute | solution.py:187
  19.4 27.0 %all-to-all-start = ((bf16[16,128,256]{2,1,0:T(8,128)(2,1)}), bf16[16,128,256]{2,1,0:T(8,128)(2,1)S(1)}, u32[]{:S(2)}, u32[]{:S(2)}) async-start(bf16[16,128,256]{2,1,0:T(8,128)(2,1)} %shard_map.48), calls=%async_computation | async-start | bytes 2097152 | tf_op jit(solution)/shard_map/all_to_all | solution.py:179
  26.8 19.6 %collective-permute-start.2 = (bf16[128,1024]{1,0:T(8,128)(2,1)S(1)}, bf16[128,1024]{1,0:T(8,128)(2,1)S(1)}, u32[]{:S(2)}, u32[]{:S(2)}) collective-permute-start(bf16[128,1024]{1,0:T(8,128)(2,1)S(1)} %get-tuple-element.28), channel_id=1, source_target_pairs={{0,4},{1,5},{2,6},{3,7},{4,8},{5,9},{6,10},{7,11},{8,12},{9,13},{1... | collective-permute-start | bytes 786440 | tf_op jit(solution)/shard_map/ppermute | solution.py:193
  30.2 16.2 %collective-permute-start.3 = (bf16[128,1024]{1,0:T(8,128)(2,1)S(1)}, bf16[128,1024]{1,0:T(8,128)(2,1)S(1)}, u32[]{:S(2)}, u32[]{:S(2)}) collective-permute-start(bf16[128,1024]{1,0:T(8,128)(2,1)S(1)} %get-tuple-element.29), channel_id=1, source_target_pairs={{0,12},{1,13},{2,14},{3,15},{4,0},{5,1},{6,2},{7,3},{8,4},{9,5},{1... | collective-permute-start | bytes 786440 | tf_op jit(solution)/shard_map/ppermute | solution.py:193
  35.0 17.2 %copy-start.1 = (s32[1,256,2]{1,2,0:T(2,128)S(1)}, s32[1,256,2]{1,2,0:T(2,128)}, u32[]{:S(2)}) copy-start(s32[1,256,2]{1,2,0:T(2,128)} %param.7) | copy-start | bytes 6148
  46.4 21.3 %all-to-all-start.1 = ((bf16[16,128,256]{2,1,0:T(8,128)(2,1)}), bf16[16,128,256]{2,1,0:T(8,128)(2,1)S(1)}, u32[]{:S(2)}, u32[]{:S(2)}) async-start(bf16[16,128,256]{2,1,0:T(8,128)(2,1)} %shard_map.46), calls=%async_computation.1 | async-start | bytes 2097152 | tf_op jit(solution)/shard_map/all_to_all | solution.py:179
  52.3 9.6 %collective-permute-start = (s32[32,8]{1,0:T(8,128)S(1)}, s32[32,8]{1,0:T(8,128)S(1)}, u32[]{:S(2)}, u32[]{:S(2)}) collective-permute-start(s32[32,8]{1,0:T(8,128)S(1)} %reshape_squeeze.3), channel_id=1, source_target_pairs={{0,480},{1,481},{2,482},{3,483},{4,484},{5,485},{6,486},{7,487},{8... | collective-permute-start | bytes 3080 | tf_op jit(solution)/shard_map/ppermute | solution.py:188
  56.9 15.6 %collective-permute-start.4 = (bf16[128,1024]{1,0:T(8,128)(2,1)S(1)}, bf16[128,1024]{1,0:T(8,128)(2,1)}, u32[]{:S(2)}, u32[]{:S(2)}) collective-permute-start(bf16[128,1024]{1,0:T(8,128)(2,1)S(1)} %get-tuple-element.37), channel_id=1, source_target_pairs={{0,8},{1,9},{2,10},{3,11},{4,12},{5,13},{6,14},{7,15},{8,0},{9,1},... | collective-permute-start | bytes 786440 | tf_op jit(solution)/shard_map/ppermute | solution.py:193
  76.7 14.3 %collective-permute-start.5 = (bf16[128,1024]{1,0:T(8,128)(2,1)S(1)}, bf16[128,1024]{1,0:T(8,128)(2,1)S(1)}, u32[]{:S(2)}, u32[]{:S(2)}) collective-permute-start(bf16[128,1024]{1,0:T(8,128)(2,1)S(1)} %get-tuple-element.39), channel_id=1, source_target_pairs={{0,32},{1,33},{2,34},{3,35},{4,36},{5,37},{6,38},{7,39},{8,40},{9,... | collective-permute-start | bytes 786440 | tf_op jit(solution)/shard_map/ppermute | solution.py:207
  78.6 16.9 %collective-permute-start.7 = (bf16[128,1024]{1,0:T(8,128)(2,1)S(1)}, bf16[128,1024]{1,0:T(8,128)(2,1)S(1)}, u32[]{:S(2)}, u32[]{:S(2)}) collective-permute-start(bf16[128,1024]{1,0:T(8,128)(2,1)S(1)} %get-tuple-element.40), channel_id=1, source_target_pairs={{0,40},{1,41},{2,42},{3,43},{4,44},{5,45},{6,46},{7,47},{8,32},{9,... | collective-permute-start | bytes 786440 | tf_op jit(solution)/shard_map/ppermute | solution.py:207
  81.9 15.3 %collective-permute-start.6 = (bf16[128,1024]{1,0:T(8,128)(2,1)S(1)}, bf16[128,1024]{1,0:T(8,128)(2,1)S(1)}, u32[]{:S(2)}, u32[]{:S(2)}) collective-permute-start(bf16[128,1024]{1,0:T(8,128)(2,1)S(1)} %get-tuple-element.34), channel_id=1, source_target_pairs={{0,44},{1,45},{2,46},{3,47},{4,32},{5,33},{6,34},{7,35},{8,36},{9,... | collective-permute-start | bytes 786440 | tf_op jit(solution)/shard_map/ppermute | solution.py:207
  86.5 16.4 %collective-permute-start.8 = (bf16[128,1024]{1,0:T(8,128)(2,1)S(1)}, bf16[128,1024]{1,0:T(8,128)(2,1)S(1)}, u32[]{:S(2)}, u32[]{:S(2)}) collective-permute-start(bf16[128,1024]{1,0:T(8,128)(2,1)S(1)} %get-tuple-element.35), channel_id=1, source_target_pairs={{0,36},{1,37},{2,38},{3,39},{4,40},{5,41},{6,42},{7,43},{8,44},{9,... | collective-permute-start | bytes 786440 | tf_op jit(solution)/shard_map/ppermute | solution.py:207
